TPU v7x, 256 devices: a whole 4x4x8 slice. The times are simulated.
256 devices in a mesh: mem: 4 (over z_hi), tile: 64 (over y, z_lo, x, core).
Axes of the slice: x: 4, y: 4, z: 8 (z_hi: 4, z_lo: 2; z = z_hi * 2 + z_lo), core: 2. Of those that a mesh axis runs over, the one named last changes fastest.
Arguments:
- alpha: float32 [32, 8, 1536, 384], P('mem', None, 'tile'), may hold values from -6 to 6
- ensemble: bfloat16 [2, 32, 8, 1536, 384], P(None, 'mem', None, 'tile'), may hold values from -1 to 1
- innovation: float32 [2, 8, 1536, 384], P(None, None, 'tile'), may hold values from -6 to 6
- precision: float32 [2, 8, 1536, 384], P(None, None, 'tile'), may hold values from 0.5 to 8
- diffusivity: float32 [2, 8, 1536, 384], P(None, None, 'tile'), may hold values from 0.01 to 0.48, as said below
Outputs:
- gradient: float32 [32, 8, 1536, 384], P('mem', None, 'tile')
- increment: float32 [2, 8, 1536, 384], P(None, None, 'tile')
Inputs may be any that keep to these rules, and one draw needn't show every extreme that they name: diffusivity[0] lies between 0.40 and 0.48 and diffusivity[1] between 0.01 and 0.02, so the four faces of a cell sum to at most 1.
All inputs are finite; a program needn't handle non-finite values.
Results may differ from a plain program's by a relative error of at most 0.0003.
Values sent between devices are 32-bit elements; how exact they have to be, the bound alone decides.
No kernel may reach another device: no remote copies, remote signals or barrier semaphores. Data moves between devices by JAX's collectives and lax.ppermute only.
A program may use at most 64 MiB of HBM per device.

v0:
```python
import jax
import jax.numpy as jnp
from jax import lax
from jax.sharding import PartitionSpec as P

STEPS = 4


def passed_along(shard, axis, by):
    size = lax.axis_size(axis)
    return lax.ppermute(shard, axis, [(i, (i + by) % size) for i in range(size)])


def extended(cells, sides, width):
    for axis, dim in sides:
        count = lax.axis_size(axis)
        head = lax.slice_in_dim(cells, 0, width, axis=dim)
        tail = lax.slice_in_dim(cells, cells.shape[dim] - width, cells.shape[dim], axis=dim)
        cells = jnp.concatenate(
            [
                lax.ppermute(tail, axis, [(i, (i + 1) % count) for i in range(count)]),
                cells,
                lax.ppermute(head, axis, [((i + 1) % count, i) for i in range(count)]),
            ],
            axis=dim,
        )
    return cells


def diffuse(field, coeffs):
    columns = field.shape[2]
    zonal_face = coeffs[0, :, 0 : columns - 1]
    merid_face = coeffs[1, :, 1 : columns - 1]
    zonal_flux = zonal_face * (field[:, :, 1:] - field[:, :, :-1])
    interior = field[:, :, 1:-1]
    merid_flux = merid_face[:, :, :-1] * (interior[:, :, :, 1:] - interior[:, :, :, :-1])
    padding = jnp.zeros_like(interior[:, :, :, :1])
    north_flux = jnp.concatenate([merid_flux, padding], axis=3)
    south_flux = jnp.concatenate([padding, merid_flux], axis=3)
    field = interior + zonal_flux[:, :, 1:] - zonal_flux[:, :, :-1] + north_flux - south_flux
    return field


def per_device(alpha, ensemble, innovation, precision, diffusivity):
    last_column = diffusivity[0:1, :, -1:, :]
    left_column = passed_along(last_column, "tile", 1)
    left_pair = jnp.concatenate([left_column, left_column], axis=0)
    coeffs = jnp.concatenate([left_pair, diffusivity], axis=2)
    localized = alpha
    for sweep in range(STEPS):
        padded = extended(localized, (("tile", 2),), 1)
        localized = diffuse(padded, coeffs)
    partial_sum = jnp.sum(ensemble.astype(jnp.float32) * localized[None], axis=1)
    increment = lax.psum(partial_sum, "mem")
    weighted = precision * (increment - innovation)
    projected = jnp.sum(ensemble.astype(jnp.float32) * weighted[:, None], axis=0)
    adjoint_field = projected
    for sweep in range(STEPS):
        padded_adj = extended(adjoint_field, (("tile", 2),), 1)
        adjoint_field = diffuse(padded_adj, coeffs)
    gradient = alpha + adjoint_field
    return (gradient, increment)


def solution(mesh):
    in_specs = (
        P("mem", None, "tile", None),
        P(None, "mem", None, "tile", None),
        P(None, None, "tile", None),
        P(None, None, "tile", None),
        P(None, None, "tile", None),
    )
    out_specs = (P("mem", None, "tile", None), P(None, None, "tile", None))
    return jax.shard_map(
        per_device, mesh=mesh, in_specs=in_specs, out_specs=out_specs, check_vma=False
    )
```

profile of v0, /device:TPU:0, one launch (start us, length us, event | category | flops | bytes accessed | tf_op | source)
XLA Modules:
  0.0 170.2 jit_solution(2937847615105471655)
XLA Ops:
  8.2 1.5 fusion.42
  9.8 6.0 %collective-permute-start.1 = (f32[8,8,1,384]{3,1,2,0:T(8,128)S(1)}, f32[8,8,1,384]{3,1,2,0:T(8,128)S(1)}, u32[]{:S(2)}, u32[]{:S(2)}) collective-permute-start(f32[8,8,1,384]{3,1,2,0:T(8,128)S(1)} %copy.56), channel_id=1, source_target_pairs={{1,0},{2,1},{3,2},{4,3},{5,4},{6,5},{7,6},{8,7},{9,8},{10,9},{11,1... | collective-permute-start | bytes 294920 | tf_op jit(solution)/shard_map/ppermute | solution.py:23
  16.9 3.2 %subtract_multiply_fusion = f32[8,8,24,383]{3,2,1,0:T(8,128)S(1)} fusion(f32[8,8,24,384]{3,2,1,0:T(8,128)} %param.5, f32[8,24,383]{2,1,0:T(8,128)S(1)} %bitcast.5), kind=kLoop, calls=%fused_computation.67 | loop fusion | flops 1176576 | bytes 7353600 | tf_op jit(solution)/shard_map/mul | solution.py:36
  20.3 3.8 %collective-permute-done.2 = f32[8,8,1,384]{3,1,2,0:T(8,128)S(1)} collective-permute-done((f32[8,8,1,384]{3,1,2,0:T(8,128)S(1)}, f32[8,8,1,384]{3,1,2,0:T(8,128)S(1)}, u32[]{:S(2)}, u32[]{:S(2)}) %collective-permute-start.2) | collective-permute-done | bytes 98336 | tf_op jit(solution)/shard_map/ppermute | solution.py:21
  24.8 1.0 fusion.33
  26.0 2.2 %collective-permute-start.3 = (f32[8,8,1,384]{3,1,2,0:T(8,128)S(1)}, f32[8,8,1,384]{3,1,2,0:T(8,128)S(1)}, u32[]{:S(2)}, u32[]{:S(2)}) collective-permute-start(f32[8,8,1,384]{3,1,2,0:T(8,128)S(1)} %copy.27), channel_id=1, source_target_pairs={{1,0},{2,1},{3,2},{4,3},{5,4},{6,5},{7,6},{8,7},{9,8},{10,9},{11,1... | collective-permute-start | bytes 294920 | tf_op jit(solution)/shard_map/ppermute | solution.py:23
  29.0 1.4 collective-permute-done.3
  30.5 6.0 %collective-permute-done.4 = f32[8,8,1,384]{3,1,2,0:T(8,128)S(1)} collective-permute-done((f32[8,8,1,384]{3,1,2,0:T(8,128)S(1)}, f32[8,8,1,384]{3,1,2,0:T(8,128)S(1)}, u32[]{:S(2)}, u32[]{:S(2)}) %collective-permute-start.4) | collective-permute-done | bytes 98336 | tf_op jit(solution)/shard_map/ppermute | solution.py:21
  37.2 1.0 fusion.31
  40.8 6.2 %collective-permute-done.6 = f32[8,8,1,384]{3,1,2,0:T(8,128)S(1)} collective-permute-done((f32[8,8,1,384]{3,1,2,0:T(8,128)S(1)}, f32[8,8,1,384]{3,1,2,0:T(8,128)S(1)}, u32[]{:S(2)}, u32[]{:S(2)}) %collective-permute-start.6) | collective-permute-done | bytes 98336 | tf_op jit(solution)/shard_map/ppermute | solution.py:21
  47.7 1.0 fusion.28
  51.3 6.0 %collective-permute-done.8 = f32[8,8,1,384]{3,1,2,0:T(8,128)S(1)} collective-permute-done((f32[8,8,1,384]{3,1,2,0:T(8,128)S(1)}, f32[8,8,1,384]{3,1,2,0:T(8,128)S(1)}, u32[]{:S(2)}, u32[]{:S(2)}) %collective-permute-start.8) | collective-permute-done | bytes 98336 | tf_op jit(solution)/shard_map/ppermute | solution.py:21
  58.0 1.0 fusion.25
  59.6 1.3 fusion
  61.0 51.2 %all-reduce.18.cloned.1.call-done = f32[2,8,24,384]{3,2,1,0:T(8,128)} async-done(((f32[2,8,24,384]{3,2,1,0:T(8,128)}), f32[2,8,24,384]{3,2,1,0:T(8,128)}) %all-reduce.18.cloned.1.call-update) | async-done | bytes 589840 | tf_op jit(solution)/shard_map/psum | solution.py:54
  112.2 1.6 subtract_multiply_fusion.1
  115.1 4.3 %collective-permute-start.9 = (f32[8,8,1,384]{3,1,2,0:T(8,128)S(1)}, f32[8,8,1,384]{3,1,2,0:T(8,128)S(1)}, u32[]{:S(2)}, u32[]{:S(2)}) collective-permute-start(f32[8,8,1,384]{3,1,2,0:T(8,128)S(1)} %copy.39), channel_id=1, source_target_pairs={{1,0},{2,1},{3,2},{4,3},{5,4},{6,5},{7,6},{8,7},{9,8},{10,9},{11,1... | collective-permute-start | bytes 294920 | tf_op jit(solution)/shard_map/ppermute | solution.py:23
  120.4 1.2 collective-permute-done.9
  121.7 6.2 %collective-permute-done.10 = f32[8,8,1,384]{3,1,2,0:T(8,128)S(1)} collective-permute-done((f32[8,8,1,384]{3,1,2,0:T(8,128)S(1)}, f32[8,8,1,384]{3,1,2,0:T(8,128)S(1)}, u32[]{:S(2)}, u32[]{:S(2)}) %collective-permute-start.10) | collective-permute-done | bytes 98336 | tf_op jit(solution)/shard_map/ppermute | solution.py:21
  132.2 6.0 %collective-permute-done.12 = f32[8,8,1,384]{3,1,2,0:T(8,128)S(1)} collective-permute-done((f32[8,8,1,384]{3,1,2,0:T(8,128)S(1)}, f32[8,8,1,384]{3,1,2,0:T(8,128)S(1)}, u32[]{:S(2)}, u32[]{:S(2)}) %collective-permute-start.12) | collective-permute-done | bytes 98336 | tf_op jit(solution)/shard_map/ppermute | solution.py:21
  142.4 6.0 %collective-permute-done.14 = f32[8,8,1,384]{3,1,2,0:T(8,128)S(1)} collective-permute-done((f32[8,8,1,384]{3,1,2,0:T(8,128)S(1)}, f32[8,8,1,384]{3,1,2,0:T(8,128)S(1)}, u32[]{:S(2)}, u32[]{:S(2)}) %collective-permute-start.14) | collective-permute-done | bytes 98336 | tf_op jit(solution)/shard_map/ppermute | solution.py:21
  149.1 1.3 fusion.16
  153.0 6.3 %collective-permute-done.16 = f32[8,8,1,384]{3,1,2,0:T(8,128)S(1)} collective-permute-done((f32[8,8,1,384]{3,1,2,0:T(8,128)S(1)}, f32[8,8,1,384]{3,1,2,0:T(8,128)S(1)}, u32[]{:S(2)}, u32[]{:S(2)}) %collective-permute-start.16) | collective-permute-done | bytes 98336 | tf_op jit(solution)/shard_map/ppermute | solution.py:21
  160.0 2.6 %fusion.13 = f32[8,8,24,384]{3,2,1,0:T(8,128)} fusion(f32[8,8,24,384]{3,2,1,0:T(8,128)S(1)} %copy-done, f32[8,8,25,384]{3,2,1,0:T(8,128)S(1)} %fusion.9, f32[8,8,24,384]{3,2,1,0:T(8,128)S(1)} %fusion.16, f32[8,8,24,383]{3,2,1,0:T(8,128)S(1)} %fusion.10), kind=kLoop, calls=%fused_computation.25 | loop fusion | flops 2949120 | bytes 14149632 | tf_op jit(solution)/shard_map/add | solution.py:61
  (97 shorter events, 26.9 us)
Async XLA Ops:
  7.2 105.0 %all-reduce.18.cloned.1.call-start = ((), (), s32[]{:S(2)}) async-start(), calls=%async_computation | async-start | bytes 1179648 | tf_op jit(solution)/shard_map/psum | solution.py:54
  8.1 12.0 %collective-permute-start = (f32[1,8,1,384]{3,1,2,0:T(8,128)S(1)}, f32[1,8,1,384]{3,1,2,0:T(8,128)S(1)}, u32[]{:S(2)}, u32[]{:S(2)}) collective-permute-start(f32[1,8,1,384]{3,1,2,0:T(8,128)S(1)} %copy.55), channel_id=1, source_target_pairs={{0,1},{1,2},{2,3},{3,4},{4,5},{5,6},{6,7},{7,8},{8,9},{9,10},{10,1... | collective-permute-start | bytes 36872 | tf_op jit(solution)/shard_map/ppermute | solution.py:11
  9.8 10.5 %collective-permute-start.1 = (f32[8,8,1,384]{3,1,2,0:T(8,128)S(1)}, f32[8,8,1,384]{3,1,2,0:T(8,128)S(1)}, u32[]{:S(2)}, u32[]{:S(2)}) collective-permute-start(f32[8,8,1,384]{3,1,2,0:T(8,128)S(1)} %copy.56), channel_id=1, source_target_pairs={{1,0},{2,1},{3,2},{4,3},{5,4},{6,5},{7,6},{8,7},{9,8},{10,9},{11,1... | collective-permute-start | bytes 294920 | tf_op jit(solution)/shard_map/ppermute | solution.py:23
  15.8 8.3 %collective-permute-start.2 = (f32[8,8,1,384]{3,1,2,0:T(8,128)S(1)}, f32[8,8,1,384]{3,1,2,0:T(8,128)S(1)}, u32[]{:S(2)}, u32[]{:S(2)}) collective-permute-start(f32[8,8,1,384]{3,1,2,0:T(8,128)S(1)} %copy.57), channel_id=1, source_target_pairs={{0,1},{1,2},{2,3},{3,4},{4,5},{5,6},{6,7},{7,8},{8,9},{9,10},{10,1... | collective-permute-start | bytes 294920 | tf_op jit(solution)/shard_map/ppermute | solution.py:21
  16.9 3.3 %copy-start.4 = (f32[2,8,24,384]{3,2,1,0:T(8,128)S(1)}, f32[2,8,24,384]{3,2,1,0:T(8,128)}, u32[]{:S(2)}) copy-start(f32[2,8,24,384]{3,2,1,0:T(8,128)} %param.9) | copy-start | bytes 1769476
  16.9 7.4 %copy-start = (f32[8,8,24,384]{3,2,1,0:T(8,128)S(1)}, f32[8,8,24,384]{3,2,1,0:T(8,128)}, u32[]{:S(2)}) copy-start(f32[8,8,24,384]{3,2,1,0:T(8,128)} %param.5) | copy-start | bytes 7077892
  26.0 4.5 %collective-permute-start.3 = (f32[8,8,1,384]{3,1,2,0:T(8,128)S(1)}, f32[8,8,1,384]{3,1,2,0:T(8,128)S(1)}, u32[]{:S(2)}, u32[]{:S(2)}) collective-permute-start(f32[8,8,1,384]{3,1,2,0:T(8,128)S(1)} %copy.27), channel_id=1, source_target_pairs={{1,0},{2,1},{3,2},{4,3},{5,4},{6,5},{7,6},{8,7},{9,8},{10,9},{11,1... | collective-permute-start | bytes 294920 | tf_op jit(solution)/shard_map/ppermute | solution.py:23
  28.2 8.3 %collective-permute-start.4 = (f32[8,8,1,384]{3,1,2,0:T(8,128)S(1)}, f32[8,8,1,384]{3,1,2,0:T(8,128)S(1)}, u32[]{:S(2)}, u32[]{:S(2)}) collective-permute-start(f32[8,8,1,384]{3,1,2,0:T(8,128)S(1)} %copy.29), channel_id=1, source_target_pairs={{0,1},{1,2},{2,3},{3,4},{4,5},{5,6},{6,7},{7,8},{8,9},{9,10},{10,1... | collective-permute-start | bytes 294920 | tf_op jit(solution)/shard_map/ppermute | solution.py:21
  38.4 2.3 %collective-permute-start.5 = (f32[8,8,1,384]{3,1,2,0:T(8,128)S(1)}, f32[8,8,1,384]{3,1,2,0:T(8,128)S(1)}, u32[]{:S(2)}, u32[]{:S(2)}) collective-permute-start(f32[8,8,1,384]{3,1,2,0:T(8,128)S(1)} %copy.31), channel_id=1, source_target_pairs={{1,0},{2,1},{3,2},{4,3},{5,4},{6,5},{7,6},{8,7},{9,8},{10,9},{11,1... | collective-permute-start | bytes 294920 | tf_op jit(solution)/shard_map/ppermute | solution.py:23
  38.5 8.5 %collective-permute-start.6 = (f32[8,8,1,384]{3,1,2,0:T(8,128)S(1)}, f32[8,8,1,384]{3,1,2,0:T(8,128)S(1)}, u32[]{:S(2)}, u32[]{:S(2)}) collective-permute-start(f32[8,8,1,384]{3,1,2,0:T(8,128)S(1)} %copy.33), channel_id=1, source_target_pairs={{0,1},{1,2},{2,3},{3,4},{4,5},{5,6},{6,7},{7,8},{8,9},{9,10},{10,1... | collective-permute-start | bytes 294920 | tf_op jit(solution)/shard_map/ppermute | solution.py:21
  48.9 2.3 %collective-permute-start.7 = (f32[8,8,1,384]{3,1,2,0:T(8,128)S(1)}, f32[8,8,1,384]{3,1,2,0:T(8,128)S(1)}, u32[]{:S(2)}, u32[]{:S(2)}) collective-permute-start(f32[8,8,1,384]{3,1,2,0:T(8,128)S(1)} %copy.35), channel_id=1, source_target_pairs={{1,0},{2,1},{3,2},{4,3},{5,4},{6,5},{7,6},{8,7},{9,8},{10,9},{11,1... | collective-permute-start | bytes 294920 | tf_op jit(solution)/shard_map/ppermute | solution.py:23
  49.0 8.3 %collective-permute-start.8 = (f32[8,8,1,384]{3,1,2,0:T(8,128)S(1)}, f32[8,8,1,384]{3,1,2,0:T(8,128)S(1)}, u32[]{:S(2)}, u32[]{:S(2)}) collective-permute-start(f32[8,8,1,384]{3,1,2,0:T(8,128)S(1)} %copy.37), channel_id=1, source_target_pairs={{0,1},{1,2},{2,3},{3,4},{4,5},{5,6},{6,7},{7,8},{8,9},{9,10},{10,1... | collective-permute-start | bytes 294920 | tf_op jit(solution)/shard_map/ppermute | solution.py:21
  57.9 1.7 copy-start.1
  112.2 2.2 %copy-start.2 = (bf16[2,8,8,24,384]{4,3,2,1,0:T(8,128)(2,1)S(1)}, bf16[2,8,8,24,384]{4,3,2,1,0:T(8,128)(2,1)}, u32[]{:S(2)}) copy-start(bf16[2,8,8,24,384]{4,3,2,1,0:T(8,128)(2,1)} %param.6) | copy-start | bytes 7077892
  115.1 6.5 %collective-permute-start.9 = (f32[8,8,1,384]{3,1,2,0:T(8,128)S(1)}, f32[8,8,1,384]{3,1,2,0:T(8,128)S(1)}, u32[]{:S(2)}, u32[]{:S(2)}) collective-permute-start(f32[8,8,1,384]{3,1,2,0:T(8,128)S(1)} %copy.39), channel_id=1, source_target_pairs={{1,0},{2,1},{3,2},{4,3},{5,4},{6,5},{7,6},{8,7},{9,8},{10,9},{11,1... | collective-permute-start | bytes 294920 | tf_op jit(solution)/shard_map/ppermute | solution.py:23
  119.4 8.6 %collective-permute-start.10 = (f32[8,8,1,384]{3,1,2,0:T(8,128)S(1)}, f32[8,8,1,384]{3,1,2,0:T(8,128)S(1)}, u32[]{:S(2)}, u32[]{:S(2)}) collective-permute-start(f32[8,8,1,384]{3,1,2,0:T(8,128)S(1)} %copy.41), channel_id=1, source_target_pairs={{0,1},{1,2},{2,3},{3,4},{4,5},{5,6},{6,7},{7,8},{8,9},{9,10},{10,1... | collective-permute-start | bytes 294920 | tf_op jit(solution)/shard_map/ppermute | solution.py:21
  129.7 2.3 %collective-permute-start.11 = (f32[8,8,1,384]{3,1,2,0:T(8,128)S(1)}, f32[8,8,1,384]{3,1,2,0:T(8,128)S(1)}, u32[]{:S(2)}, u32[]{:S(2)}) collective-permute-start(f32[8,8,1,384]{3,1,2,0:T(8,128)S(1)} %copy.43), channel_id=1, source_target_pairs={{1,0},{2,1},{3,2},{4,3},{5,4},{6,5},{7,6},{8,7},{9,8},{10,9},{11,1... | collective-permute-start | bytes 294920 | tf_op jit(solution)/shard_map/ppermute | solution.py:23
  129.9 8.3 %collective-permute-start.12 = (f32[8,8,1,384]{3,1,2,0:T(8,128)S(1)}, f32[8,8,1,384]{3,1,2,0:T(8,128)S(1)}, u32[]{:S(2)}, u32[]{:S(2)}) collective-permute-start(f32[8,8,1,384]{3,1,2,0:T(8,128)S(1)} %copy.45), channel_id=1, source_target_pairs={{0,1},{1,2},{2,3},{3,4},{4,5},{5,6},{6,7},{7,8},{8,9},{9,10},{10,1... | collective-permute-start | bytes 294920 | tf_op jit(solution)/shard_map/ppermute | solution.py:21
  140.0 2.3 %collective-permute-start.13 = (f32[8,8,1,384]{3,1,2,0:T(8,128)S(1)}, f32[8,8,1,384]{3,1,2,0:T(8,128)S(1)}, u32[]{:S(2)}, u32[]{:S(2)}) collective-permute-start(f32[8,8,1,384]{3,1,2,0:T(8,128)S(1)} %copy.47), channel_id=1, source_target_pairs={{1,0},{2,1},{3,2},{4,3},{5,4},{6,5},{7,6},{8,7},{9,8},{10,9},{11,1... | collective-permute-start | bytes 294920 | tf_op jit(solution)/shard_map/ppermute | solution.py:23
  140.1 8.3 %collective-permute-start.14 = (f32[8,8,1,384]{3,1,2,0:T(8,128)S(1)}, f32[8,8,1,384]{3,1,2,0:T(8,128)S(1)}, u32[]{:S(2)}, u32[]{:S(2)}) collective-permute-start(f32[8,8,1,384]{3,1,2,0:T(8,128)S(1)} %copy.49), channel_id=1, source_target_pairs={{0,1},{1,2},{2,3},{3,4},{4,5},{5,6},{6,7},{7,8},{8,9},{9,10},{10,1... | collective-permute-start | bytes 294920 | tf_op jit(solution)/shard_map/ppermute | solution.py:21
  150.6 2.3 %collective-permute-start.15 = (f32[8,8,1,384]{3,1,2,0:T(8,128)S(1)}, f32[8,8,1,384]{3,1,2,0:T(8,128)S(1)}, u32[]{:S(2)}, u32[]{:S(2)}) collective-permute-start(f32[8,8,1,384]{3,1,2,0:T(8,128)S(1)} %copy.51), channel_id=1, source_target_pairs={{1,0},{2,1},{3,2},{4,3},{5,4},{6,5},{7,6},{8,7},{9,8},{10,9},{11,1... | collective-permute-start | bytes 294920 | tf_op jit(solution)/shard_map/ppermute | solution.py:23
  150.7 8.6 %collective-permute-start.16 = (f32[8,8,1,384]{3,1,2,0:T(8,128)S(1)}, f32[8,8,1,384]{3,1,2,0:T(8,128)S(1)}, u32[]{:S(2)}, u32[]{:S(2)}) collective-permute-start(f32[8,8,1,384]{3,1,2,0:T(8,128)S(1)} %copy.53), channel_id=1, source_target_pairs={{0,1},{1,2},{2,3},{3,4},{4,5},{5,6},{6,7},{7,8},{8,9},{9,10},{10,1... | collective-permute-start | bytes 294920 | tf_op jit(solution)/shard_map/ppermute | solution.py:21
  159.9 2.6 %copy-start.3 = (f32[2,8,24,384]{3,2,1,0:T(8,128)S(1)}, f32[2,8,24,384]{3,2,1,0:T(8,128)}, u32[]{:S(2)}) copy-start(f32[2,8,24,384]{3,2,1,0:T(8,128)} %all-reduce.18.cloned.1.call-done) | copy-start | bytes 1769476
Sparse Core Ops, SparseCore 0:
  61.1 51.0 all-reduce.17
where the time goes:
time: 170 us
  waiting for transfers between devices  105 us (62%)
  other arithmetic  25.7 us (15%)
  starting transfers between devices  16.8 us (10%)
  between operations  14.5 us (9%)
  local copies, waits for them, and re-layouts  8.15 us (5%)
    psum x1, waiting for transfers between devices, per_device(): increment = lax.psum(partial_sum, 'mem')  51.2 us
    ppermute x8, waiting for transfers between devices, extended(): lax.ppermute(tail, axis, [(i, (i + 1) % count) for i in range(count)])  46.7 us
    ppermute x8, starting transfers between devices, extended(): lax.ppermute(head, axis, [((i + 1) % count, i) for i in range(count)])  13 us
    mul x8, other arithmetic, diffuse(): merid_face[:, :, :-1] * (interior[:, :, :, 1:] - interior[:, :, :, :-1])  7.93 us
    sub x7, other arithmetic, diffuse(): interior + zonal_flux[:, :, 1:] - zonal_flux[:, :, :-1] + north_flux  7.44 us
    ppermute x8, waiting for transfers between devices, extended(): lax.ppermute(head, axis, [((i + 1) % count, i) for i in range(count)])  7.04 us
    mul x9, other arithmetic, diffuse(): zonal_flux = zonal_face * (field[:, :, 1:] - field[:, :, :-1])  4.29 us
    ppermute x8, starting transfers between devices, extended(): lax.ppermute(tail, axis, [(i, (i + 1) % count) for i in range(count)])  3.67 us
  transfers between devices with their start and end apart: 18, of which 16 were waited for; matrix products, arithmetic and copies ran while one was open for 7% of the time, Pallas kernels for 0%

commit v1 on v0

v1 whole, which is shorter than its diff:
```python
import jax
import jax.numpy as jnp
from jax import lax
from jax.experimental import pallas as pl
from jax.experimental.pallas import tpu as pltpu
from jax.sharding import PartitionSpec as P

STEPS = 4
HALO = 4
TILE_ROWS = 8
VMEM_BYTES = 48 * 1024 * 1024


def shifted(values, by, axis):
    return pltpu.roll(values, by % values.shape[axis], axis)


def low_half(shape):
    return lax.broadcasted_iota(jnp.int32, shape, len(shape) - 2) < HALO


def masked_rows(face):
    last = lax.broadcasted_iota(jnp.int32, face.shape, 1) == face.shape[1] - 1
    return jnp.where(last, 0.0, face)


def diffuse(field, zonal, merid):
    for sweep in range(STEPS):
        zonal_flux = zonal * (shifted(field, -1, 0) - field)
        merid_flux = merid * (shifted(field, -1, 1) - field)
        field = field + (zonal_flux - shifted(zonal_flux, 1, 0))
        field = field + (merid_flux - shifted(merid_flux, 1, 1))
    return field


def paired_heads(first, second):
    return jnp.where(low_half(first.shape), first, shifted(second, HALO, 0))


def paired_tails(first, second):
    return jnp.where(low_half(first.shape), shifted(first, HALO, 0), second)


def halo_tiles(from_left, from_right):
    low = low_half(from_left.shape)
    first = jnp.where(low, from_right, shifted(from_left, HALO, 0))
    second = jnp.where(low, shifted(from_right, HALO, 0), from_left)
    return first, second


def pack_controls(alpha_lo, alpha_hi, coeffs_lo, coeffs_hi, head, tail):
    members = alpha_lo.shape[0]
    for m in range(members):
        head[m, 0] = paired_heads(alpha_lo[m, 0], alpha_lo[m, 1])
        tail[m, 0] = paired_tails(alpha_hi[m, 0], alpha_hi[m, 1])
    for f in range(2):
        head[members + f, 0] = paired_heads(coeffs_lo[f, 0], coeffs_lo[f, 1])
        tail[members + f, 0] = paired_tails(coeffs_hi[f, 0], coeffs_hi[f, 1])


def pack_ensemble(ensemble, head, tail):
    slots, members = ensemble.shape[:2]

    def one(m, carry):
        for t in range(slots):
            first = ensemble[t, m, 0].astype(jnp.float32)
            second = ensemble[t, m, 1].astype(jnp.float32)
            head[t, m, 0] = paired_heads(first[:8], second[:8])
            tail[t, m, 0] = paired_tails(first[16:], second[16:])
        return carry

    lax.fori_loop(0, members, one, 0)


def localize_interior(alpha, ensemble, coeffs, out):
    members = alpha.shape[0]
    zonal = coeffs[0, 0]
    merid = masked_rows(coeffs[1, 0])
    low = low_half((TILE_ROWS, alpha.shape[3]))

    def one(m, sums):
        field = diffuse(alpha[m, 0], zonal, merid)
        return tuple(
            total + ensemble[t, m, 0].astype(jnp.float32) * field for t, total in enumerate(sums)
        )

    zero = jnp.zeros(alpha.shape[2:], jnp.float32)
    sums = lax.fori_loop(0, members, one, (zero, zero))
    for t, total in enumerate(sums):
        out[t, 0, :8] = total[8:16]
        out[t, 0, 8:] = jnp.where(low, total[16:], total[:8])


def edge_slabs(hi, lo, left, right):
    first, second = halo_tiles(left, right)
    return (
        jnp.concatenate([hi[0], first, lo[0]], axis=0),
        jnp.concatenate([hi[1], second, lo[1]], axis=0),
    )


def edge_coeffs(coeffs_lo, coeffs_hi, left, right, base):
    zonal = edge_slabs(coeffs_hi[0], coeffs_lo[0], left[base, 0], right[base, 0])
    merid = edge_slabs(coeffs_hi[1], coeffs_lo[1], left[base + 1, 0], right[base + 1, 0])
    return zonal, tuple(masked_rows(face) for face in merid)


def localize_edges(alpha_lo, alpha_hi, ensemble, coeffs_lo, coeffs_hi, left, right, out):
    members = alpha_lo.shape[0]
    zonal, merid = edge_coeffs(coeffs_lo, coeffs_hi, left, right, members)
    low = low_half((TILE_ROWS, out.shape[3]))

    def one(m, sums):
        slabs = edge_slabs(alpha_hi[m], alpha_lo[m], left[m, 0], right[m, 0])
        new = []
        for j in range(2):
            field = diffuse(slabs[j], zonal[j], merid[j])
            edge = jnp.where(low, field[16:], field[:8])
            for t in range(2):
                scale = ensemble[t, m, j].astype(jnp.float32)
                new.append(sums[2 * j + t] + jnp.where(low, scale[:8], scale[16:]) * edge)
        return tuple(new)

    zero = jnp.zeros(out.shape[2:], jnp.float32)
    sums = lax.fori_loop(0, members, one, (zero,) * 4)
    for j in range(2):
        for t in range(2):
            out[t, j] = sums[2 * j + t]


def weigh_edges(mine, other, innov_lo, innov_hi, prec_lo, prec_hi, head, tail):
    low = low_half((TILE_ROWS, mine.shape[3]))
    for t in range(2):
        edges = []
        for j in range(2):
            innovation = jnp.where(low, innov_lo[t, j], innov_hi[t, j])
            precision = jnp.where(low, prec_lo[t, j], prec_hi[t, j])
            edges.append(precision * (mine[t, j] + other[t, j] - innovation))
        head[t, 0] = paired_heads(edges[0], edges[1])
        tail[t, 0] = paired_tails(edges[0], edges[1])


def adjoint_interior(
    mine, other, mine_edge, other_edge, innovation, precision, ensemble, alpha, coeffs,
    increment, weighted, inner,
):
    members = alpha.shape[0]
    low = low_half((TILE_ROWS, alpha.shape[3]))
    zonal = coeffs[0, 0]
    merid = masked_rows(coeffs[1, 0])
    weights = []
    for t in range(2):
        middle = mine[t, 0] + other[t, 0]
        edge = mine_edge[t, 0] + other_edge[t, 0]
        rest = middle[8:]
        total = jnp.concatenate(
            [jnp.where(low, edge, rest), middle[:8], jnp.where(low, rest, edge)], axis=0
        )
        increment[t, 0] = total
        weights.append(precision[t, 0] * (total - innovation[t, 0]))
        weighted[t, 0] = weights[t]

    def one(m, carry):
        projected = ensemble[0, m, 0].astype(jnp.float32) * weights[0]
        projected = projected + ensemble[1, m, 0].astype(jnp.float32) * weights[1]
        inner[m, 0] = alpha[m, 0] + diffuse(projected, zonal, merid)
        return carry

    lax.fori_loop(0, members, one, 0)


def adjoint_edges(
    inner, alpha_lo, alpha_hi, ensemble, ens_left, ens_right, weighted, w_left, w_right,
    coeffs_lo, coeffs_hi, left, right, gradient,
):
    members = inner.shape[0]
    low = low_half((TILE_ROWS, inner.shape[3]))
    zonal, merid = edge_coeffs(coeffs_lo, coeffs_hi, left, right, members)

    def one(m, carry):
        halo_left = ens_left[0, m, 0] * w_left[0, 0] + ens_left[1, m, 0] * w_left[1, 0]
        halo_right = ens_right[0, m, 0] * w_right[0, 0] + ens_right[1, m, 0] * w_right[1, 0]
        halos = halo_tiles(halo_left, halo_right)
        for j in range(2):
            projected = ensemble[0, m, j].astype(jnp.float32) * weighted[0, j]
            projected = projected + ensemble[1, m, j].astype(jnp.float32) * weighted[1, j]
            slab = jnp.concatenate([projected[16:], halos[j], projected[:8]], axis=0)
            field = diffuse(slab, zonal[j], merid[j])
            gradient[m, j, :8] = jnp.where(low, alpha_lo[m, j] + field[16:], inner[m, j, :8])
            gradient[m, j, 8:16] = inner[m, j, 8:16]
            gradient[m, j, 16:] = jnp.where(low, inner[m, j, 16:], alpha_hi[m, j] + field[:8])
        return carry

    lax.fori_loop(0, members, one, 0)


def block(shape, dims, at=0):
    walk, step = dims
    sizes = tuple(step if d == walk else n for d, n in enumerate(shape))
    return pl.BlockSpec(sizes, lambda i: tuple(i if d == walk else 0 for d in range(len(shape))))


def rows8(shape, dims, at):
    walk, step = dims
    sizes = tuple(step if d == walk else n for d, n in enumerate(shape[:2 + len(shape) - 4]))
    sizes = sizes + (TILE_ROWS, shape[-1])
    last = len(shape) - 2
    return pl.BlockSpec(
        sizes, lambda i: tuple(i if d == walk else at if d == last else 0 for d in range(len(shape)))
    )


def f32(*shape):
    return jax.ShapeDtypeStruct(shape, jnp.float32)


def run(kernel, grid, in_specs, out_specs, out_shape, flops, *args):
    read = sum(a.size * a.dtype.itemsize for a in args)
    wrote = sum(4 * s.size for s in jax.tree.leaves(out_shape))
    return pl.pallas_call(
        kernel,
        grid=(grid,),
        in_specs=in_specs,
        out_specs=out_specs,
        out_shape=out_shape,
        cost_estimate=pl.CostEstimate(flops=flops, bytes_accessed=read + wrote, transcendentals=0),
        compiler_params=pltpu.CompilerParams(vmem_limit_bytes=VMEM_BYTES),
    )(*args)


def to_right(value):
    size = lax.axis_size("tile")
    return lax.ppermute(value, "tile", [(i, (i + 1) % size) for i in range(size)])


def to_left(value):
    size = lax.axis_size("tile")
    return lax.ppermute(value, "tile", [(i, (i - 1) % size) for i in range(size)])


def with_partner(value, first):
    mem, tile = lax.axis_size("mem"), lax.axis_size("tile")
    pairs = []
    for m in range(mem):
        for t in range(tile):
            flip = 1 if (t % 2 == 0) == first else 3
            pairs.append((m * tile + t, (m ^ flip) * tile + t))
    return lax.ppermute(value, ("mem", "tile"), pairs)


def per_device(alpha, ensemble, innovation, precision, diffusivity):
    members, levels, columns, rows = alpha.shape
    slots = ensemble.shape[0]
    pairs = levels // 2
    work = members * levels * columns * rows * 10 * STEPS

    a_lo, a_hi = (rows8(alpha.shape, (1, 2), at) for at in (0, 2))
    c_lo, c_hi = (rows8(diffusivity.shape, (1, 2), at) for at in (0, 2))
    edge = f32(members + 2, pairs, TILE_ROWS, rows)
    edge_spec = block(edge.shape, (1, 1))
    head, tail = run(
        pack_controls, pairs, [a_lo, a_hi, c_lo, c_hi], [edge_spec] * 2, [edge] * 2, 0,
        alpha, alpha, diffusivity, diffusivity,
    )
    left = to_right(tail)
    right = to_left(head)

    mid = f32(slots, levels, 16, rows)
    part_mid = run(
        localize_interior, levels,
        [block(alpha.shape, (1, 1)), block(ensemble.shape, (2, 1)), block(diffusivity.shape, (1, 1))],
        block(mid.shape, (1, 1)), mid, work, alpha, ensemble, diffusivity,
    )
    got_mid = with_partner(part_mid, True)

    ens_edge = f32(slots, members, pairs, TILE_ROWS, rows)
    ens_edge_spec = block(ens_edge.shape, (2, 1))
    ens_head, ens_tail = run(
        pack_ensemble, pairs, [block(ensemble.shape, (2, 2))], [ens_edge_spec] * 2, [ens_edge] * 2, 0,
        ensemble,
    )

    rim = f32(slots, levels, TILE_ROWS, rows)
    part_rim = run(
        localize_edges, pairs,
        [a_lo, a_hi, block(ensemble.shape, (2, 2)), c_lo, c_hi, edge_spec, edge_spec],
        block(rim.shape, (1, 2)), rim, work,
        alpha, alpha, ensemble, diffusivity, diffusivity, left, right,
    )
    got_rim = with_partner(part_rim, True)
    half_mid = part_mid + got_mid
    other_mid = with_partner(half_mid, False)
    half_rim = part_rim + got_rim
    other_rim = with_partner(half_rim, False)
    ens_left = to_right(ens_tail)
    ens_right = to_left(ens_head)

    o_lo, o_hi = (rows8(innovation.shape, (1, 2), at) for at in (0, 2))
    w_edge = f32(slots, pairs, TILE_ROWS, rows)
    w_edge_spec = block(w_edge.shape, (1, 1))
    rim_spec = block(rim.shape, (1, 2))
    w_head, w_tail = run(
        weigh_edges, pairs, [rim_spec, rim_spec, o_lo, o_hi, o_lo, o_hi],
        [w_edge_spec] * 2, [w_edge] * 2, 0,
        half_rim, other_rim, innovation, innovation, precision, precision,
    )
    w_left = to_right(w_tail)
    w_right = to_left(w_head)

    obs = f32(*innovation.shape)
    obs_spec = block(obs.shape, (1, 1))
    mid_spec, rim1_spec = block(mid.shape, (1, 1)), block(rim.shape, (1, 1))
    field = f32(*alpha.shape)
    field_spec = block(alpha.shape, (1, 1))
    increment, weighted, inner = run(
        adjoint_interior, levels,
        [mid_spec, mid_spec, rim1_spec, rim1_spec, obs_spec, obs_spec,
         block(ensemble.shape, (2, 1)), field_spec, block(diffusivity.shape, (1, 1))],
        [obs_spec, obs_spec, field_spec], [obs, obs, field], work,
        half_mid, other_mid, half_rim, other_rim, innovation, precision, ensemble, alpha, diffusivity,
    )

    field2_spec = block(alpha.shape, (1, 2))
    gradient = run(
        adjoint_edges, pairs,
        [field2_spec, a_lo, a_hi, block(ensemble.shape, (2, 2)), ens_edge_spec, ens_edge_spec,
         block(obs.shape, (1, 2)), w_edge_spec, w_edge_spec, c_lo, c_hi, edge_spec, edge_spec],
        field2_spec, field, work,
        inner, alpha, alpha, ensemble, ens_left, ens_right, weighted, w_left, w_right,
        diffusivity, diffusivity, left, right,
    )
    return (gradient, increment)


def solution(mesh):
    in_specs = (
        P("mem", None, "tile", None),
        P(None, "mem", None, "tile", None),
        P(None, None, "tile", None),
        P(None, None, "tile", None),
        P(None, None, "tile", None),
    )
    out_specs = (P("mem", None, "tile", None), P(None, None, "tile", None))
    return jax.shard_map(
        per_device, mesh=mesh, in_specs=in_specs, out_specs=out_specs, check_vma=False
    )
```

time: 170 us -> 174 us (1.024)
  Pallas kernels: 0 us -> 125 us
  waiting for transfers between devices: 105 us -> 16.8 us
  other arithmetic: 25.7 us -> 0.07 us
  between operations: 14.5 us -> 0.77 us
  starting transfers between devices: 16.8 us -> 26.5 us
  local copies, waits for them, and re-layouts: 8.15 us -> 4.18 us
    pallas_call x0 -> x7, Pallas kernels: none -> 125 us  [run(): pl.pallas_call(kernel, grid=(grid,), in_specs=in_specs, out_specs=out_spe...]
    psum x1 -> x0, waiting for transfers between devices: 51.2 us -> none  [per_device(): increment = lax.psum(partial_sum, 'mem')]
    ppermute x17 -> x10, waiting for transfers between devices: 53.7 us -> 16.8 us  [the longest x4 16.8 us: with_partner(): return lax.ppermute(value, ('mem', 'tile'), pairs)]
    mul x18 -> x0, other arithmetic: 13.9 us -> none  [the longest x8 7.93 us: diffuse(): merid_face[:, :, :-1] * (interior[:, :, :, 1:] - interior[:, :, :, :-1])]
    ppermute x17 -> x10, starting transfers between devices: 16.8 us -> 26.5 us  [the longest x3 17.8 us: to_left(): lax.ppermute(value, 'tile', [(i, (i - 1) % size) for i in range(size)])]
    sub x7 -> x0, other arithmetic: 7.44 us -> none  [diffuse(): interior + zonal_flux[:, :, 1:] - zonal_flux[:, :, :-1] + north_flux]
    slice x23 -> x0, local copies, waits for them, and re-layouts: 3.5 us -> none  [the longest x15 2.53 us: extended(): lax.slice_in_dim(cells, cells.shape[dim] - width, cells.shape[dim], axis=...]
    add x1 -> x2, other arithmetic: 2.59 us -> 0.07 us  [the longest x1 0.05 us: per_device(): half_mid = part_mid + got_mid]
  transfers between devices with their start and end apart: 18 -> 10, of which waited for: 16 -> 2; matrix products, arithmetic and copies ran while one was open for 7% -> 0% of each run, Pallas kernels for 0% -> 59%
where the time goes in v1:
time: 174 us
  Pallas kernels  125 us (72%)
  starting transfers between devices  26.5 us (15%)
  waiting for transfers between devices  16.8 us (10%)
  local copies, waits for them, and re-layouts  4.18 us (2%)
    pallas_call x7, Pallas kernels, run(): pl.pallas_call(kernel, grid=(grid,), in_specs=in_specs, out_specs=out_spe...  125 us
    ppermute x3, starting transfers between devices, to_left(): lax.ppermute(value, 'tile', [(i, (i - 1) % size) for i in range(size)])  17.8 us
    ppermute x4, waiting for transfers between devices, with_partner(): return lax.ppermute(value, ('mem', 'tile'), pairs)  16.8 us
    ppermute x4, starting transfers between devices, with_partner(): return lax.ppermute(value, ('mem', 'tile'), pairs)  8.44 us
    unnamed x16, local copies, waits for them, and re-layouts  4.18 us
  transfers between devices with their start and end apart: 10, of which 2 were waited for; matrix products, arithmetic and copies ran while one was open for 0% of the time, Pallas kernels for 59%

profile of v1, /device:TPU:0, one launch (start us, length us, event | category | flops | bytes accessed | tf_op | source)
XLA Modules:
  0.0 173.7 jit_solution(8798565634148372248)
XLA Ops:
  0.6 0.0 copy-start
  0.6 1.7 copy-done
  2.3 1.1 copy-done.3
  3.4 0.4 shard_map.69
  3.8 0.1 collective-permute-start.2
  3.9 6.0 %collective-permute-start.3 = (f32[10,4,8,384]{3,2,1,0:T(8,128)S(1)}, f32[10,4,8,384]{3,2,1,0:T(8,128)S(1)}, u32[]{:S(2)}, u32[]{:S(2)}) collective-permute-start(f32[10,4,8,384]{3,2,1,0:T(8,128)S(1)} %get-tuple-element.12), channel_id=1, source_target_pairs={{0,63},{1,0},{2,1},{3,2},{4,3},{5,4},{6,5},{7,6},{8,7},{9,8},{10,9... | collective-permute-start | bytes 1474568 | tf_op jit(solution)/shard_map/ppermute | solution.py:238
  9.8 39.6 %shard_map.68 = f32[2,8,16,384]{3,2,1,0:T(8,128)S(1)} custom-call(f32[8,8,24,384]{3,2,1,0:T(8,128)S(1)} %copy-done, bf16[2,8,8,24,384]{4,3,2,1,0:T(8,128)(2,1)S(1)} %copy-done.2, f32[2,8,24,384]{3,2,1,0:T(8,128)S(1)} %copy-done.3), custom_call_target="tpu_custom_call" | custom-call | flops 23592960 | bytes 5701632 | tf_op jit(solution)/shard_map/pallas_call | solution.py:220
  49.5 1.7 %collective-permute-start = (f32[2,8,16,384]{3,2,1,0:T(8,128)S(1)}, f32[2,8,16,384]{3,2,1,0:T(8,128)S(1)}, u32[]{:S(2)}, u32[]{:S(2)}) collective-permute-start(f32[2,8,16,384]{3,2,1,0:T(8,128)S(1)} %shard_map.68), channel_id=1, source_target_pairs={{0,64},{1,193},{2,66},{3,195},{4,68},{5,197},{6,70},{7,199},{8,72}... | collective-permute-start | bytes 1179656 | tf_op jit(solution)/shard_map/ppermute | solution.py:248
  51.2 0.8 shard_map.72
  52.0 0.1 collective-permute-start.6
  52.1 0.0 copy-start.5
  52.1 5.9 %collective-permute-start.7 = (f32[2,8,4,8,384]{4,3,2,1,0:T(8,128)S(1)}, f32[2,8,4,8,384]{4,3,2,1,0:T(8,128)S(1)}, u32[]{:S(2)}, u32[]{:S(2)}) collective-permute-start(f32[2,8,4,8,384]{4,3,2,1,0:T(8,128)S(1)} %get-tuple-element.15), channel_id=1, source_target_pairs={{0,63},{1,0},{2,1},{3,2},{4,3},{5,4},{6,5},{7,6},{8,7},{9,8},{10,9... | collective-permute-start | bytes 2359304 | tf_op jit(solution)/shard_map/ppermute | solution.py:238
  58.1 20.5 %shard_map.70 = f32[2,8,8,384]{3,2,1,0:T(8,128)S(1)} custom-call(f32[8,8,24,384]{3,2,1,0:T(8,128)S(1)} %copy-done.1, f32[8,8,24,384]{3,2,1,0:T(8,128)S(1)} %copy-done.1, bf16[2,8,8,24,384]{4,3,2,1,0:T(8,128)(2,1)} %ensemble.9, f32[2,8,24,384]{3,2,1,0:T(8,128)S(1)} %copy-done.4, f32[2,8,24,384]{3,2,1,0:T(8,128)S(1)} %copy-done.4, ...), custom_call_target="tpu_custom_call" | custom-call | flops 23592960 | bytes 9437184 | tf_op jit(solution)/shard_map/pallas_call | solution.py:220
  78.6 1.4 collective-permute-start.4
  80.0 4.7 %collective-permute-start.1 = (f32[2,8,16,384]{3,2,1,0:T(8,128)S(1)}, f32[2,8,16,384]{3,2,1,0:T(8,128)S(1)}, u32[]{:S(2)}, u32[]{:S(2)}) collective-permute-start(f32[2,8,16,384]{3,2,1,0:T(8,128)S(1)} %add.6.mine), channel_id=1, source_target_pairs={{0,192},{1,65},{2,194},{3,67},{4,196},{5,69},{6,198},{7,71},{8,200... | collective-permute-start | bytes 1179656 | tf_op jit(solution)/shard_map/ppermute | solution.py:248
  84.7 9.6 %collective-permute-done.4 = f32[2,8,8,384]{3,2,1,0:T(8,128)S(1)} collective-permute-done((f32[2,8,8,384]{3,2,1,0:T(8,128)S(1)}, f32[2,8,8,384]{3,2,1,0:T(8,128)S(1)}, u32[]{:S(2)}, u32[]{:S(2)}) %collective-permute-start.4) | collective-permute-done | bytes 196640 | tf_op jit(solution)/shard_map/ppermute | solution.py:248
  94.3 0.7 collective-permute-start.5
  95.0 7.2 %collective-permute-done.5.other_edge.other = f32[2,8,8,384]{3,2,1,0:T(8,128)S(1)} collective-permute-done((f32[2,8,8,384]{3,2,1,0:T(8,128)S(1)}, f32[2,8,8,384]{3,2,1,0:T(8,128)S(1)}, u32[]{:S(2)}, u32[]{:S(2)}) %collective-permute-start.5) | collective-permute-done | bytes 196640 | tf_op jit(solution)/shard_map/ppermute | solution.py:248
  102.2 0.3 shard_map.73
  102.5 0.1 collective-permute-start.8
  102.6 6.0 %collective-permute-start.9 = (f32[2,4,8,384]{3,2,1,0:T(8,128)S(1)}, f32[2,4,8,384]{3,2,1,0:T(8,128)S(1)}, u32[]{:S(2)}, u32[]{:S(2)}) collective-permute-start(f32[2,4,8,384]{3,2,1,0:T(8,128)S(1)} %get-tuple-element.18), channel_id=1, source_target_pairs={{0,63},{1,0},{2,1},{3,2},{4,3},{5,4},{6,5},{7,6},{8,7},{9,8},{10,9... | collective-permute-start | bytes 294920 | tf_op jit(solution)/shard_map/ppermute | solution.py:238
  108.6 41.6 %shard_map.71 = (f32[2,8,24,384]{3,2,1,0:T(8,128)}, f32[2,8,24,384]{3,2,1,0:T(8,128)S(1)}, f32[8,8,24,384]{3,2,1,0:T(8,128)S(1)}) custom-call(f32[2,8,16,384]{3,2,1,0:T(8,128)S(1)} %add.6.mine, f32[2,8,16,384]{3,2,1,0:T(8,128)S(1)} %collective-permute-done.1.other, f32[2,8,8,384]{3,2,1,0:T(8,128)S(1)} %add.7.mine_edge.mine, ...), custom_call_target="tpu_custom_call" | custom-call | flops 23592960 | bytes 11206656 | tf_op jit(solution)/shard_map/pallas_call | solution.py:220
  150.2 1.4 copy-done.7
  151.7 22.0 %shard_map.74 = f32[8,8,24,384]{3,2,1,0:T(8,128)} custom-call(f32[8,8,24,384]{3,2,1,0:T(8,128)} %copy-done.7, f32[8,8,24,384]{3,2,1,0:T(8,128)} %alpha_hi.5, f32[8,8,24,384]{3,2,1,0:T(8,128)} %alpha_hi.5, bf16[2,8,8,24,384]{4,3,2,1,0:T(8,128)(2,1)} %ensemble.9, f32[2,8,4,8,384]{4,3,2,1,0:T(8,128)S(1)} %collective-permute-done.6.ens_left, ...), custom_call_target="tpu_custom_call" | custom-call | flops 23592960 | bytes 16318464 | tf_op jit(solution)/shard_map/pallas_call | solution.py:220
  (21 shorter events, 0.1 us)
Async XLA Ops:
  0.6 1.7 copy-start
  2.3 1.1 copy-start.3
  3.4 6.5 %copy-start.2 = (bf16[2,8,8,24,384]{4,3,2,1,0:T(8,128)(2,1)S(1)}, bf16[2,8,8,24,384]{4,3,2,1,0:T(8,128)(2,1)}, u32[]{:S(2)}) copy-start(bf16[2,8,8,24,384]{4,3,2,1,0:T(8,128)(2,1)} %ensemble.9) | copy-start | bytes 7077892
  3.8 54.3 %collective-permute-start.2 = (f32[10,4,8,384]{3,2,1,0:T(8,128)S(1)}, f32[10,4,8,384]{3,2,1,0:T(8,128)S(1)}, u32[]{:S(2)}, u32[]{:S(2)}) collective-permute-start(f32[10,4,8,384]{3,2,1,0:T(8,128)S(1)} %get-tuple-element.11), channel_id=1, source_target_pairs={{0,1},{1,2},{2,3},{3,4},{4,5},{5,6},{6,7},{7,8},{8,9},{9,10},{10,1... | collective-permute-start | bytes 1474568 | tf_op jit(solution)/shard_map/ppermute | solution.py:233
  3.9 54.2 %collective-permute-start.3 = (f32[10,4,8,384]{3,2,1,0:T(8,128)S(1)}, f32[10,4,8,384]{3,2,1,0:T(8,128)S(1)}, u32[]{:S(2)}, u32[]{:S(2)}) collective-permute-start(f32[10,4,8,384]{3,2,1,0:T(8,128)S(1)} %get-tuple-element.12), channel_id=1, source_target_pairs={{0,63},{1,0},{2,1},{3,2},{4,3},{5,4},{6,5},{7,6},{8,7},{9,8},{10,9... | collective-permute-start | bytes 1474568 | tf_op jit(solution)/shard_map/ppermute | solution.py:238
  9.8 48.2 %copy-start.4 = (f32[2,8,24,384]{3,2,1,0:T(8,128)S(1)}, f32[2,8,24,384]{3,2,1,0:T(8,128)}, u32[]{:S(2)}) copy-start(f32[2,8,24,384]{3,2,1,0:T(8,128)} %coeffs_hi.5) | copy-start | bytes 1769476
  49.5 8.6 %copy-start.1 = (f32[8,8,24,384]{3,2,1,0:T(8,128)S(1)}, f32[8,8,24,384]{3,2,1,0:T(8,128)}, u32[]{:S(2)}) copy-start(f32[8,8,24,384]{3,2,1,0:T(8,128)} %alpha_hi.5) | copy-start | bytes 7077892
  49.5 30.5 %collective-permute-start = (f32[2,8,16,384]{3,2,1,0:T(8,128)S(1)}, f32[2,8,16,384]{3,2,1,0:T(8,128)S(1)}, u32[]{:S(2)}, u32[]{:S(2)}) collective-permute-start(f32[2,8,16,384]{3,2,1,0:T(8,128)S(1)} %shard_map.68), channel_id=1, source_target_pairs={{0,64},{1,193},{2,66},{3,195},{4,68},{5,197},{6,70},{7,199},{8,72}... | collective-permute-start | bytes 1179656 | tf_op jit(solution)/shard_map/ppermute | solution.py:248
  52.0 99.7 %collective-permute-start.6 = (f32[2,8,4,8,384]{4,3,2,1,0:T(8,128)S(1)}, f32[2,8,4,8,384]{4,3,2,1,0:T(8,128)S(1)}, u32[]{:S(2)}, u32[]{:S(2)}) collective-permute-start(f32[2,8,4,8,384]{4,3,2,1,0:T(8,128)S(1)} %get-tuple-element.14), channel_id=1, source_target_pairs={{0,1},{1,2},{2,3},{3,4},{4,5},{5,6},{6,7},{7,8},{8,9},{9,10},{10,1... | collective-permute-start | bytes 2359304 | tf_op jit(solution)/shard_map/ppermute | solution.py:233
  52.1 50.1 %copy-start.5 = (f32[2,8,24,384]{3,2,1,0:T(8,128)S(1)}, f32[2,8,24,384]{3,2,1,0:T(8,128)}, u32[]{:S(2)}) copy-start(f32[2,8,24,384]{3,2,1,0:T(8,128)} %innov_hi.1) | copy-start | bytes 1769476
  52.1 50.1 %copy-start.6 = (f32[2,8,24,384]{3,2,1,0:T(8,128)S(1)}, f32[2,8,24,384]{3,2,1,0:T(8,128)}, u32[]{:S(2)}) copy-start(f32[2,8,24,384]{3,2,1,0:T(8,128)} %prec_hi.1) | copy-start | bytes 1769476
  52.1 99.5 %collective-permute-start.7 = (f32[2,8,4,8,384]{4,3,2,1,0:T(8,128)S(1)}, f32[2,8,4,8,384]{4,3,2,1,0:T(8,128)S(1)}, u32[]{:S(2)}, u32[]{:S(2)}) collective-permute-start(f32[2,8,4,8,384]{4,3,2,1,0:T(8,128)S(1)} %get-tuple-element.15), channel_id=1, source_target_pairs={{0,63},{1,0},{2,1},{3,2},{4,3},{5,4},{6,5},{7,6},{8,7},{9,8},{10,9... | collective-permute-start | bytes 2359304 | tf_op jit(solution)/shard_map/ppermute | solution.py:238
  78.6 15.7 %collective-permute-start.4 = (f32[2,8,8,384]{3,2,1,0:T(8,128)S(1)}, f32[2,8,8,384]{3,2,1,0:T(8,128)S(1)}, u32[]{:S(2)}, u32[]{:S(2)}) collective-permute-start(f32[2,8,8,384]{3,2,1,0:T(8,128)S(1)} %shard_map.70), channel_id=1, source_target_pairs={{0,64},{1,193},{2,66},{3,195},{4,68},{5,197},{6,70},{7,199},{8,72}... | collective-permute-start | bytes 589832 | tf_op jit(solution)/shard_map/ppermute | solution.py:248
  80.0 28.6 %collective-permute-start.1 = (f32[2,8,16,384]{3,2,1,0:T(8,128)S(1)}, f32[2,8,16,384]{3,2,1,0:T(8,128)S(1)}, u32[]{:S(2)}, u32[]{:S(2)}) collective-permute-start(f32[2,8,16,384]{3,2,1,0:T(8,128)S(1)} %add.6.mine), channel_id=1, source_target_pairs={{0,192},{1,65},{2,194},{3,67},{4,196},{5,69},{6,198},{7,71},{8,200... | collective-permute-start | bytes 1179656 | tf_op jit(solution)/shard_map/ppermute | solution.py:248
  94.3 7.9 %collective-permute-start.5 = (f32[2,8,8,384]{3,2,1,0:T(8,128)S(1)}, f32[2,8,8,384]{3,2,1,0:T(8,128)S(1)}, u32[]{:S(2)}, u32[]{:S(2)}) collective-permute-start(f32[2,8,8,384]{3,2,1,0:T(8,128)S(1)} %add.7.mine_edge.mine), channel_id=1, source_target_pairs={{0,192},{1,65},{2,194},{3,67},{4,196},{5,69},{6,198},{7,71},{8,200... | collective-permute-start | bytes 589832 | tf_op jit(solution)/shard_map/ppermute | solution.py:248
  102.5 49.1 %collective-permute-start.8 = (f32[2,4,8,384]{3,2,1,0:T(8,128)S(1)}, f32[2,4,8,384]{3,2,1,0:T(8,128)S(1)}, u32[]{:S(2)}, u32[]{:S(2)}) collective-permute-start(f32[2,4,8,384]{3,2,1,0:T(8,128)S(1)} %get-tuple-element.17), channel_id=1, source_target_pairs={{0,1},{1,2},{2,3},{3,4},{4,5},{5,6},{6,7},{7,8},{8,9},{9,10},{10,1... | collective-permute-start | bytes 294920 | tf_op jit(solution)/shard_map/ppermute | solution.py:233
  102.6 49.1 %collective-permute-start.9 = (f32[2,4,8,384]{3,2,1,0:T(8,128)S(1)}, f32[2,4,8,384]{3,2,1,0:T(8,128)S(1)}, u32[]{:S(2)}, u32[]{:S(2)}) collective-permute-start(f32[2,4,8,384]{3,2,1,0:T(8,128)S(1)} %get-tuple-element.18), channel_id=1, source_target_pairs={{0,63},{1,0},{2,1},{3,2},{4,3},{5,4},{6,5},{7,6},{8,7},{9,8},{10,9... | collective-permute-start | bytes 294920 | tf_op jit(solution)/shard_map/ppermute | solution.py:238
  150.2 1.4 copy-start.7

commit v2 on v1

v2 whole, which is shorter than its diff:
```python
import jax
import jax.numpy as jnp
from jax import lax
from jax.experimental import pallas as pl
from jax.experimental.pallas import tpu as pltpu
from jax.sharding import PartitionSpec as P

STEPS = 4
HALO = 4
TILE_ROWS = 8
VMEM_BYTES = 48 * 1024 * 1024


def shifted(values, by, axis):
    return pltpu.roll(values, by % values.shape[axis], axis)


def low_half(shape):
    return lax.broadcasted_iota(jnp.int32, shape, len(shape) - 2) < HALO


def masked_rows(face):
    last = lax.broadcasted_iota(jnp.int32, face.shape, 1) == face.shape[1] - 1
    return jnp.where(last, 0.0, face)


def diffuse(fields, zonal, merid):
    rows = lax.broadcasted_iota(jnp.int32, (TILE_ROWS, zonal.shape[1]), 0)
    kept = [None] * len(fields)
    for sweep in range(STEPS):
        zonal_flux = [zonal * (shifted(f, -1, 0) - f) for f in fields]
        merid_flux = [merid * (shifted(f, -1, 1) - f) for f in fields]
        inward = [shifted(z, 1, 0) for z in zonal_flux]
        for i, f in enumerate(fields):
            cell = jnp.where(rows < HALO, f[:8], f[16:])
            flux = jnp.where(rows < HALO, zonal_flux[i][:8], inward[i][16:])
            if sweep:
                mine = (rows == sweep) | (rows == 7 - sweep)
                cell = jnp.where(mine, cell, kept[i][0])
                flux = jnp.where(mine, flux, kept[i][1])
            kept[i] = (cell, flux)
        fields = [
            (f + (z - w)) + (g - shifted(g, 1, 1))
            for f, z, w, g in zip(fields, zonal_flux, inward, merid_flux)
        ]
    return fields, kept


def window(outer, inner, by, side):
    if by == 0:
        return outer
    rows = lax.broadcasted_iota(jnp.int32, outer.shape, 0) % HALO
    if side == 0:
        return jnp.where(rows < HALO - by, shifted(outer, -by, 0), shifted(inner, HALO - by, 0))
    return jnp.where(rows >= by, shifted(outer, by, 0), shifted(inner, by - HALO, 0))


def edge_windows(outer, own, side):
    zonal_at = 0 if side == 0 else 1
    steps = []
    for step in range(STEPS):
        zonal = window(outer[0], own[0], step + zonal_at, side)
        merid = window(outer[1], own[1], step + 1, side)
        steps.append((zonal, masked_rows(merid)))
    return steps


def diffuse_edges(halos, kept, windows, side):
    rows = lax.broadcasted_iota(jnp.int32, halos[0].shape, 0) % HALO
    inward = -1 if side == 0 else 1
    newest = rows == (HALO - 1 if side == 0 else 0)
    outer = halos
    for step in range(STEPS):
        zonal, merid = windows[step]
        turn = -inward * (HALO - 1 - step)
        cells, flux_in = [], []
        for previous, (cell, flux) in zip(outer, kept):
            cells.append(jnp.where(newest, shifted(cell, turn, 0), shifted(previous, inward, 0)))
            flux_in.append(shifted(flux, turn, 0))
        merid_flux = [merid * (shifted(c, -1, 1) - c) for c in cells]
        after = []
        for previous, cell, flux, g in zip(outer, cells, flux_in, merid_flux):
            out_flux = zonal * (cell - previous if side == 0 else previous - cell)
            in_flux = jnp.where(newest, flux, shifted(out_flux, inward, 0))
            change = in_flux - out_flux if side == 0 else out_flux - in_flux
            after.append((cell + change) + (g - shifted(g, 1, 1)))
        outer = after
    return outer


def paired_heads(first, second):
    return jnp.where(low_half(first.shape), first, shifted(second, HALO, 0))


def paired_tails(first, second):
    return jnp.where(low_half(first.shape), shifted(first, HALO, 0), second)


def paired(first, second, side):
    return (paired_heads if side == 0 else paired_tails)(first, second)


def levels_of(left, right):
    low = low_half(left.shape)
    return (
        jnp.where(low, left, shifted(right, HALO, 0)),
        jnp.where(low, shifted(left, HALO, 0), right),
    )


def pack_controls(alpha_lo, alpha_hi, coeffs_lo, coeffs_hi, head, tail):
    members = alpha_lo.shape[0]
    for m in range(members):
        head[m, 0] = paired_heads(alpha_lo[m, 0], alpha_lo[m, 1])
        tail[m, 0] = paired_tails(alpha_hi[m, 0], alpha_hi[m, 1])
    for f in range(2):
        head[members + f, 0] = paired_heads(coeffs_lo[f, 0], coeffs_lo[f, 1])
        tail[members + f, 0] = paired_tails(coeffs_hi[f, 0], coeffs_hi[f, 1])


def pack_ensemble(ensemble, head, tail):
    slots, members = ensemble.shape[:2]

    def one(m, carry):
        for t in range(slots):
            first = ensemble[t, m, 0].astype(jnp.float32)
            second = ensemble[t, m, 1].astype(jnp.float32)
            head[t, m, 0] = paired_heads(first[:8], second[:8])
            tail[t, m, 0] = paired_tails(first[16:], second[16:])
        return carry

    lax.fori_loop(0, members, one, 0)


def keep_all(kept, cells, fluxes):
    for m, (cell, flux) in enumerate(kept):
        cells[m, 0] = cell
        fluxes[m, 0] = flux


def localize_interior(alpha, ensemble, coeffs, out, cells, fluxes):
    members = alpha.shape[0]
    low = low_half((TILE_ROWS, alpha.shape[3]))
    fields = [alpha[m, 0] for m in range(members)]
    fields, kept = diffuse(fields, coeffs[0, 0], masked_rows(coeffs[1, 0]))
    keep_all(kept, cells, fluxes)
    for t in range(2):
        total = ensemble[t, 0, 0].astype(jnp.float32) * fields[0]
        for m in range(1, members):
            total = total + ensemble[t, m, 0].astype(jnp.float32) * fields[m]
        out[t, 0, :8] = total[8:16]
        out[t, 0, 8:] = jnp.where(low, total[16:], total[:8])


def edges_of(halos, cells, fluxes, coeffs_lo, coeffs_hi, outer, base, members, side):
    own = coeffs_lo if side == 0 else coeffs_hi
    own = [paired(own[f, 0], own[f, 1], side) for f in range(2)]
    windows = edge_windows([outer[base, 0], outer[base + 1, 0]], own, side)
    kept = [
        (paired(cells[m, 0], cells[m, 1], side), paired(fluxes[m, 0], fluxes[m, 1], side))
        for m in range(members)
    ]
    return diffuse_edges([halos[m, 0] for m in range(members)], kept, windows, side)


def localize_edges(
    left, right, cells, fluxes, coeffs_lo, coeffs_hi, ens_head, ens_tail, out,
):
    members = cells.shape[0]
    for side, (outer, scale) in enumerate(((left, ens_head), (right, ens_tail))):
        edges = edges_of(
            outer, cells, fluxes, coeffs_lo, coeffs_hi, outer, members, members, side
        )
        for t in range(2):
            total = scale[t, 0, 0] * edges[0]
            for m in range(1, members):
                total = total + scale[t, m, 0] * edges[m]
            out[t, side, 0] = total


def project_edges(
    mine, other, innov_lo, innov_hi, prec_lo, prec_hi, ens_head, ens_tail, rim, head, tail
):
    members = ens_head.shape[1]
    totals = [[mine[t, side, 0] + other[t, side, 0] for side in range(2)] for t in range(2)]
    for t in range(2):
        first, second = levels_of(*totals[t])
        rim[t, 0] = first
        rim[t, 1] = second
    sides = ((innov_lo, prec_lo, ens_head, head), (innov_hi, prec_hi, ens_tail, tail))
    for side, (innov, prec, scale, out) in enumerate(sides):
        weights = [
            paired(prec[t, 0], prec[t, 1], side)
            * (totals[t][side] - paired(innov[t, 0], innov[t, 1], side))
            for t in range(2)
        ]
        for m in range(members):
            out[m, 0] = scale[0, m, 0] * weights[0] + scale[1, m, 0] * weights[1]


def adjoint_interior(
    mine, other, rim, innovation, precision, ensemble, alpha, coeffs,
    increment, inner, cells, fluxes,
):
    members = alpha.shape[0]
    low = low_half((TILE_ROWS, alpha.shape[3]))
    weights = []
    for t in range(2):
        middle = mine[t, 0] + other[t, 0]
        edge, rest = rim[t, 0], middle[8:]
        total = jnp.concatenate(
            [jnp.where(low, edge, rest), middle[:8], jnp.where(low, rest, edge)], axis=0
        )
        increment[t, 0] = total
        weights.append(precision[t, 0] * (total - innovation[t, 0]))
    projected = [
        ensemble[0, m, 0].astype(jnp.float32) * weights[0]
        + ensemble[1, m, 0].astype(jnp.float32) * weights[1]
        for m in range(members)
    ]
    fields, kept = diffuse(projected, coeffs[0, 0], masked_rows(coeffs[1, 0]))
    keep_all(kept, cells, fluxes)
    for m in range(members):
        inner[m, 0] = alpha[m, 0] + fields[m]


def adjoint_edges(
    inner, alpha_lo, alpha_hi, p_left, p_right, cells, fluxes, coeffs_lo, coeffs_hi, left, right,
    gradient,
):
    members = inner.shape[0]
    low = low_half((TILE_ROWS, inner.shape[3]))
    sides = [
        edges_of(halos, cells, fluxes, coeffs_lo, coeffs_hi, outer, members, members, side)
        for side, (halos, outer) in enumerate(((p_left, left), (p_right, right)))
    ]
    for m in range(members):
        for j, edge in enumerate(levels_of(sides[0][m], sides[1][m])):
            gradient[m, j, :8] = jnp.where(low, alpha_lo[m, j] + edge, inner[m, j, :8])
            gradient[m, j, 8:16] = inner[m, j, 8:16]
            gradient[m, j, 16:] = jnp.where(low, inner[m, j, 16:], alpha_hi[m, j] + edge)


def block(shape, dims, at=0):
    walk, step = dims
    sizes = tuple(step if d == walk else n for d, n in enumerate(shape))
    return pl.BlockSpec(sizes, lambda i: tuple(i if d == walk else 0 for d in range(len(shape))))


def rows8(shape, dims, at):
    walk, step = dims
    sizes = tuple(step if d == walk else n for d, n in enumerate(shape[:2 + len(shape) - 4]))
    sizes = sizes + (TILE_ROWS, shape[-1])
    last = len(shape) - 2
    return pl.BlockSpec(
        sizes, lambda i: tuple(i if d == walk else at if d == last else 0 for d in range(len(shape)))
    )


def f32(*shape):
    return jax.ShapeDtypeStruct(shape, jnp.float32)


def run(kernel, grid, in_specs, out_specs, out_shape, flops, *args):
    read = sum(a.size * a.dtype.itemsize for a in args)
    wrote = sum(4 * s.size for s in jax.tree.leaves(out_shape))
    return pl.pallas_call(
        kernel,
        grid=(grid,),
        in_specs=in_specs,
        out_specs=out_specs,
        out_shape=out_shape,
        cost_estimate=pl.CostEstimate(flops=flops, bytes_accessed=read + wrote, transcendentals=0),
        compiler_params=pltpu.CompilerParams(vmem_limit_bytes=VMEM_BYTES),
    )(*args)


def to_right(value):
    size = lax.axis_size("tile")
    return lax.ppermute(value, "tile", [(i, (i + 1) % size) for i in range(size)])


def to_left(value):
    size = lax.axis_size("tile")
    return lax.ppermute(value, "tile", [(i, (i - 1) % size) for i in range(size)])


def with_partner(value, first):
    mem, tile = lax.axis_size("mem"), lax.axis_size("tile")
    pairs = []
    for m in range(mem):
        for t in range(tile):
            flip = 1 if (t % 2 == 0) == first else 3
            pairs.append((m * tile + t, (m ^ flip) * tile + t))
    return lax.ppermute(value, ("mem", "tile"), pairs)


def per_device(alpha, ensemble, innovation, precision, diffusivity):
    members, levels, columns, rows = alpha.shape
    slots = ensemble.shape[0]
    pairs = levels // 2
    work = members * levels * columns * rows * 10 * STEPS

    a_lo, a_hi = (rows8(alpha.shape, (1, 2), at) for at in (0, 2))
    c_lo, c_hi = (rows8(diffusivity.shape, (1, 2), at) for at in (0, 2))
    edge = f32(members + 2, pairs, TILE_ROWS, rows)
    edge_spec = block(edge.shape, (1, 1))
    head, tail = run(
        pack_controls, pairs, [a_lo, a_hi, c_lo, c_hi], [edge_spec] * 2, [edge] * 2, 0,
        alpha, alpha, diffusivity, diffusivity,
    )
    left = to_right(tail)
    right = to_left(head)

    ens_edge = f32(slots, members, pairs, TILE_ROWS, rows)
    ens_edge_spec = block(ens_edge.shape, (2, 1))
    ens_head, ens_tail = run(
        pack_ensemble, pairs, [block(ensemble.shape, (2, 2))], [ens_edge_spec] * 2, [ens_edge] * 2, 0,
        ensemble,
    )

    mid = f32(slots, levels, 16, rows)
    mid_spec = block(mid.shape, (1, 1))
    kept = f32(members, levels, TILE_ROWS, rows)
    kept_spec = block(kept.shape, (1, 1))
    kept2_spec = block(kept.shape, (1, 2))
    field = f32(*alpha.shape)
    field_spec = block(alpha.shape, (1, 1))
    field2_spec = block(alpha.shape, (1, 2))
    ens_spec = block(ensemble.shape, (2, 1))
    coeffs_spec = block(diffusivity.shape, (1, 1))
    part_mid, cells, fluxes = run(
        localize_interior, levels, [field_spec, ens_spec, coeffs_spec],
        [mid_spec, kept_spec, kept_spec], [mid, kept, kept], work, alpha, ensemble, diffusivity,
    )
    got_mid = with_partner(part_mid, True)

    rim = f32(slots, 2, pairs, TILE_ROWS, rows)
    rim_spec = block(rim.shape, (2, 1))
    part_rim = run(
        localize_edges, pairs,
        [edge_spec, edge_spec, kept2_spec, kept2_spec, c_lo, c_hi, ens_edge_spec, ens_edge_spec],
        rim_spec, rim, work // 3,
        left, right, cells, fluxes, diffusivity, diffusivity, ens_head, ens_tail,
    )
    got_rim = with_partner(part_rim, True)
    half_mid = part_mid + got_mid
    other_mid = with_partner(half_mid, False)
    half_rim = part_rim + got_rim
    other_rim = with_partner(half_rim, False)

    o_lo, o_hi = (rows8(innovation.shape, (1, 2), at) for at in (0, 2))
    p_edge = f32(members, pairs, TILE_ROWS, rows)
    p_edge_spec = block(p_edge.shape, (1, 1))
    rim_total = f32(slots, levels, TILE_ROWS, rows)
    rim_total_spec = block(rim_total.shape, (1, 1))
    rim_total2_spec = block(rim_total.shape, (1, 2))
    total_rim, p_head, p_tail = run(
        project_edges, pairs,
        [rim_spec, rim_spec, o_lo, o_hi, o_lo, o_hi, ens_edge_spec, ens_edge_spec],
        [rim_total2_spec, p_edge_spec, p_edge_spec], [rim_total, p_edge, p_edge], 0,
        half_rim, other_rim, innovation, innovation, precision, precision, ens_head, ens_tail,
    )
    p_left = to_right(p_tail)
    p_right = to_left(p_head)

    obs = f32(*innovation.shape)
    obs_spec = block(obs.shape, (1, 1))
    increment, inner, cells, fluxes = run(
        adjoint_interior, levels,
        [mid_spec, mid_spec, rim_total_spec, obs_spec, obs_spec, ens_spec, field_spec, coeffs_spec],
        [obs_spec, field_spec, kept_spec, kept_spec], [obs, field, kept, kept], work,
        half_mid, other_mid, total_rim, innovation, precision, ensemble, alpha, diffusivity,
    )

    gradient = run(
        adjoint_edges, pairs,
        [field2_spec, a_lo, a_hi, p_edge_spec, p_edge_spec, kept2_spec, kept2_spec,
         c_lo, c_hi, edge_spec, edge_spec],
        field2_spec, field, work // 3,
        inner, alpha, alpha, p_left, p_right, cells, fluxes,
        diffusivity, diffusivity, left, right,
    )
    return (gradient, increment)


def solution(mesh):
    in_specs = (
        P("mem", None, "tile", None),
        P(None, "mem", None, "tile", None),
        P(None, None, "tile", None),
        P(None, None, "tile", None),
        P(None, None, "tile", None),
    )
    out_specs = (P("mem", None, "tile", None), P(None, None, "tile", None))
    return jax.shard_map(
        per_device, mesh=mesh, in_specs=in_specs, out_specs=out_specs, check_vma=False
    )
```

time: 174 us -> 70.1 us (0.40)
  the two profiles are of different devices: /device:TPU:0 before, /device:TPU:22 now
where the time goes in v2:
time: 70.1 us; the launch traced here: 69.5 us
  Pallas kernels  28.3 us (40%)
  waiting for transfers between devices  23.3 us (33%)
  starting transfers between devices  14.4 us (21%)
  local copies, waits for them, and re-layouts  2.75 us (4%)
  between operations  0.76 us (1%)
    pallas_call x7, Pallas kernels, run(): pl.pallas_call(kernel, grid=(grid,), in_specs=in_specs, out_specs=out_spe...  28.3 us
    ppermute x4, waiting for transfers between devices, with_partner(): return lax.ppermute(value, ('mem', 'tile'), pairs)  23.3 us
    ppermute x4, starting transfers between devices, with_partner(): return lax.ppermute(value, ('mem', 'tile'), pairs)  10.8 us
    ppermute x2, starting transfers between devices, to_left(): lax.ppermute(value, 'tile', [(i, (i - 1) % size) for i in range(size)])  3.15 us
    unnamed x12, local copies, waits for them, and re-layouts  2.75 us
  transfers between devices with their start and end apart: 8, of which 3 were waited for; matrix products, arithmetic and copies ran while one was open for 0% of the time, Pallas kernels for 32%

profile of v2, /device:TPU:22, one launch (start us, length us, event | category | flops | bytes accessed | tf_op | source)
XLA Modules:
  0.0 69.5 jit_solution(1964311639836403292)
XLA Ops:
  0.6 0.0 copy-start
  0.6 1.7 %copy-done = f32[8,8,24,384]{3,2,1,0:T(8,128)S(1)} copy-done((f32[8,8,24,384]{3,2,1,0:T(8,128)S(1)}, f32[8,8,24,384]{3,2,1,0:T(8,128)}, u32[]{:S(2)}) %copy-start) | copy-done | bytes 2359320
  2.3 1.1 %copy-done.1 = f32[2,8,24,384]{3,2,1,0:T(8,128)S(1)} copy-done((f32[2,8,24,384]{3,2,1,0:T(8,128)S(1)}, f32[2,8,24,384]{3,2,1,0:T(8,128)}, u32[]{:S(2)}) %copy-start.1) | copy-done | bytes 589848
  3.4 0.4 shard_map.69
  3.8 0.1 collective-permute-start.2
  3.9 0.0 copy-start.3
  3.9 1.7 %collective-permute-start.3 = (f32[10,4,8,384]{3,2,1,0:T(8,128)S(1)}, f32[10,4,8,384]{3,2,1,0:T(8,128)S(1)}, u32[]{:S(2)}, u32[]{:S(2)}) collective-permute-start(f32[10,4,8,384]{3,2,1,0:T(8,128)S(1)} %get-tuple-element.18), channel_id=1, source_target_pairs={{0,63},{1,0},{2,1},{3,2},{4,3},{5,4},{6,5},{7,6},{8,7},{9,8},{10,9... | collective-permute-start | bytes 1474568 | tf_op jit(solution)/shard_map/ppermute | solution.py:285
  5.6 8.2 %shard_map.68 = (f32[2,8,16,384]{3,2,1,0:T(8,128)S(1)}, f32[8,8,8,384]{3,2,1,0:T(8,128)S(1)}, f32[8,8,8,384]{3,2,1,0:T(8,128)S(1)}) custom-call(f32[8,8,24,384]{3,2,1,0:T(8,128)S(1)} %copy-done, bf16[2,8,8,24,384]{4,3,2,1,0:T(8,128)(2,1)} %ensemble.5, f32[2,8,24,384]{3,2,1,0:T(8,128)S(1)} %copy-done.1), custom_call_target="tpu_custom_call" | custom-call | flops 23592960 | bytes 7274496 | tf_op jit(solution)/shard_map/pallas_call | solution.py:267
  13.8 0.0 copy-start.2
  13.8 3.4 %collective-permute-start = (f32[2,8,16,384]{3,2,1,0:T(8,128)S(1)}, f32[2,8,16,384]{3,2,1,0:T(8,128)S(1)}, u32[]{:S(2)}, u32[]{:S(2)}) collective-permute-start(f32[2,8,16,384]{3,2,1,0:T(8,128)S(1)} %get-tuple-element.16), channel_id=1, source_target_pairs={{0,64},{1,193},{2,66},{3,195},{4,68},{5,197},{6,70},{7,199},{8,72}... | collective-permute-start | bytes 1179656 | tf_op jit(solution)/shard_map/ppermute | solution.py:295
  17.2 0.8 %shard_map.70 = (f32[2,8,4,8,384]{4,3,2,1,0:T(8,128)S(1)}, f32[2,8,4,8,384]{4,3,2,1,0:T(8,128)S(1)}) custom-call(bf16[2,8,8,24,384]{4,3,2,1,0:T(8,128)(2,1)S(1)} %copy-done.3), custom_call_target="tpu_custom_call" | custom-call | bytes 3932160 | tf_op jit(solution)/shard_map/pallas_call | solution.py:267
  18.0 0.0 copy-start.4
  18.0 3.2 %shard_map.71 = f32[2,2,4,8,384]{4,3,2,1,0:T(8,128)S(1)} custom-call(f32[10,4,8,384]{3,2,1,0:T(8,128)S(1)} %collective-permute-done.2.left, f32[10,4,8,384]{3,2,1,0:T(8,128)S(1)} %collective-permute-done.3.right, f32[8,8,8,384]{3,2,1,0:T(8,128)S(1)} %get-tuple-element.19.cells, f32[8,8,8,384]{3,2,1,0:T(8,128)S(1)} %get-tuple-element.20.fluxes, ...), custom_call_target="tpu_custom_call" | custom-call | flops 7864320 | bytes 5505024 | tf_op jit(solution)/shard_map/pallas_call | solution.py:267
  21.2 0.2 collective-permute-start.4
  21.4 9.5 %collective-permute-done.4 = f32[2,2,4,8,384]{4,3,2,1,0:T(8,128)S(1)} collective-permute-done((f32[2,2,4,8,384]{4,3,2,1,0:T(8,128)S(1)}, f32[2,2,4,8,384]{4,3,2,1,0:T(8,128)S(1)}, u32[]{:S(2)}, u32[]{:S(2)}) %collective-permute-start.4) | collective-permute-done | bytes 196640 | tf_op jit(solution)/shard_map/ppermute | solution.py:295
  30.9 7.1 %collective-permute-start.5 = (f32[2,2,4,8,384]{4,3,2,1,0:T(8,128)S(1)}, f32[2,2,4,8,384]{4,3,2,1,0:T(8,128)S(1)}, u32[]{:S(2)}, u32[]{:S(2)}) collective-permute-start(f32[2,2,4,8,384]{4,3,2,1,0:T(8,128)S(1)} %add.7.mine), channel_id=1, source_target_pairs={{0,192},{1,65},{2,194},{3,67},{4,196},{5,69},{6,198},{7,71},{8,200... | collective-permute-start | bytes 589832 | tf_op jit(solution)/shard_map/ppermute | solution.py:295
  38.1 0.1 collective-permute-start.1
  38.2 5.1 %collective-permute-done.5.other = f32[2,2,4,8,384]{4,3,2,1,0:T(8,128)S(1)} collective-permute-done((f32[2,2,4,8,384]{4,3,2,1,0:T(8,128)S(1)}, f32[2,2,4,8,384]{4,3,2,1,0:T(8,128)S(1)}, u32[]{:S(2)}, u32[]{:S(2)}) %collective-permute-start.5) | collective-permute-done | bytes 196640 | tf_op jit(solution)/shard_map/ppermute | solution.py:295
  43.3 0.6 shard_map.72
  43.9 0.4 collective-permute-start.6
  44.2 1.4 %collective-permute-start.7 = (f32[8,4,8,384]{3,2,1,0:T(8,128)S(1)}, f32[8,4,8,384]{3,2,1,0:T(8,128)S(1)}, u32[]{:S(2)}, u32[]{:S(2)}) collective-permute-start(f32[8,4,8,384]{3,2,1,0:T(8,128)S(1)} %get-tuple-element.26), channel_id=1, source_target_pairs={{0,63},{1,0},{2,1},{3,2},{4,3},{5,4},{6,5},{7,6},{8,7},{9,8},{10,9... | collective-permute-start | bytes 1179656 | tf_op jit(solution)/shard_map/ppermute | solution.py:285
  45.7 8.7 %collective-permute-done.1.other = f32[2,8,16,384]{3,2,1,0:T(8,128)S(1)} collective-permute-done((f32[2,8,16,384]{3,2,1,0:T(8,128)S(1)}, f32[2,8,16,384]{3,2,1,0:T(8,128)S(1)}, u32[]{:S(2)}, u32[]{:S(2)}) %collective-permute-start.1) | collective-permute-done | bytes 393248 | tf_op jit(solution)/shard_map/ppermute | solution.py:295
  54.3 9.5 %shard_map.73 = (f32[2,8,24,384]{3,2,1,0:T(8,128)}, f32[8,8,24,384]{3,2,1,0:T(8,128)}, f32[8,8,8,384]{3,2,1,0:T(8,128)S(1)}, f32[8,8,8,384]{3,2,1,0:T(8,128)S(1)}) custom-call(f32[2,8,16,384]{3,2,1,0:T(8,128)S(1)} %add.6.mine, f32[2,8,16,384]{3,2,1,0:T(8,128)S(1)} %collective-permute-done.1.other, f32[2,8,8,384]{3,2,1,0:T(8,128)S(1)} %get-tuple-element.23.rim, ...), custom_call_target="tpu_custom_call" | custom-call | flops 23592960 | bytes 11993088 | tf_op jit(solution)/shard_map/pallas_call | solution.py:267
  63.8 5.7 %shard_map.74 = f32[8,8,24,384]{3,2,1,0:T(8,128)} custom-call(f32[8,8,24,384]{3,2,1,0:T(8,128)} %get-tuple-element.24.inner, f32[8,8,24,384]{3,2,1,0:T(8,128)} %alpha_hi.3, f32[8,8,24,384]{3,2,1,0:T(8,128)} %alpha_hi.3, f32[8,4,8,384]{3,2,1,0:T(8,128)S(1)} %collective-permute-done.6.p_left, f32[8,4,8,384]{3,2,1,0:T(8,128)S(1)} %collective-permute-done.7.p_right, ...), custom_call_target="tpu_custom_call" | custom-call | flops 7864320 | bytes 13959168 | tf_op jit(solution)/shard_map/pallas_call | solution.py:267
  (13 shorter events, 0.1 us)
Async XLA Ops:
  0.6 1.7 %copy-start = (f32[8,8,24,384]{3,2,1,0:T(8,128)S(1)}, f32[8,8,24,384]{3,2,1,0:T(8,128)}, u32[]{:S(2)}) copy-start(f32[8,8,24,384]{3,2,1,0:T(8,128)} %alpha_hi.3) | copy-start | bytes 7077892
  2.3 1.1 %copy-start.1 = (f32[2,8,24,384]{3,2,1,0:T(8,128)S(1)}, f32[2,8,24,384]{3,2,1,0:T(8,128)}, u32[]{:S(2)}) copy-start(f32[2,8,24,384]{3,2,1,0:T(8,128)} %coeffs_hi.5) | copy-start | bytes 1769476
  3.8 14.2 %collective-permute-start.2 = (f32[10,4,8,384]{3,2,1,0:T(8,128)S(1)}, f32[10,4,8,384]{3,2,1,0:T(8,128)S(1)}, u32[]{:S(2)}, u32[]{:S(2)}) collective-permute-start(f32[10,4,8,384]{3,2,1,0:T(8,128)S(1)} %get-tuple-element.17), channel_id=1, source_target_pairs={{0,1},{1,2},{2,3},{3,4},{4,5},{5,6},{6,7},{7,8},{8,9},{9,10},{10,1... | collective-permute-start | bytes 1474568 | tf_op jit(solution)/shard_map/ppermute | solution.py:280
  3.9 13.3 %copy-start.3 = (bf16[2,8,8,24,384]{4,3,2,1,0:T(8,128)(2,1)S(1)}, bf16[2,8,8,24,384]{4,3,2,1,0:T(8,128)(2,1)}, u32[]{:S(2)}) copy-start(bf16[2,8,8,24,384]{4,3,2,1,0:T(8,128)(2,1)} %ensemble.5) | copy-start | bytes 7077892
  3.9 14.1 %collective-permute-start.3 = (f32[10,4,8,384]{3,2,1,0:T(8,128)S(1)}, f32[10,4,8,384]{3,2,1,0:T(8,128)S(1)}, u32[]{:S(2)}, u32[]{:S(2)}) collective-permute-start(f32[10,4,8,384]{3,2,1,0:T(8,128)S(1)} %get-tuple-element.18), channel_id=1, source_target_pairs={{0,63},{1,0},{2,1},{3,2},{4,3},{5,4},{6,5},{7,6},{8,7},{9,8},{10,9... | collective-permute-start | bytes 1474568 | tf_op jit(solution)/shard_map/ppermute | solution.py:285
  13.8 4.2 %copy-start.2 = (f32[2,8,24,384]{3,2,1,0:T(8,128)S(1)}, f32[2,8,24,384]{3,2,1,0:T(8,128)}, u32[]{:S(2)}) copy-start(f32[2,8,24,384]{3,2,1,0:T(8,128)} %coeffs_hi.5) | copy-start | bytes 1769476
  13.8 24.2 %collective-permute-start = (f32[2,8,16,384]{3,2,1,0:T(8,128)S(1)}, f32[2,8,16,384]{3,2,1,0:T(8,128)S(1)}, u32[]{:S(2)}, u32[]{:S(2)}) collective-permute-start(f32[2,8,16,384]{3,2,1,0:T(8,128)S(1)} %get-tuple-element.16), channel_id=1, source_target_pairs={{0,64},{1,193},{2,66},{3,195},{4,68},{5,197},{6,70},{7,199},{8,72}... | collective-permute-start | bytes 1179656 | tf_op jit(solution)/shard_map/ppermute | solution.py:295
  18.0 25.3 %copy-start.4 = (f32[2,8,24,384]{3,2,1,0:T(8,128)S(1)}, f32[2,8,24,384]{3,2,1,0:T(8,128)}, u32[]{:S(2)}) copy-start(f32[2,8,24,384]{3,2,1,0:T(8,128)} %innovation.1) | copy-start | bytes 1769476
  18.0 25.3 %copy-start.5 = (f32[2,8,24,384]{3,2,1,0:T(8,128)S(1)}, f32[2,8,24,384]{3,2,1,0:T(8,128)}, u32[]{:S(2)}) copy-start(f32[2,8,24,384]{3,2,1,0:T(8,128)} %precision.1) | copy-start | bytes 1769476
  21.2 9.7 %collective-permute-start.4 = (f32[2,2,4,8,384]{4,3,2,1,0:T(8,128)S(1)}, f32[2,2,4,8,384]{4,3,2,1,0:T(8,128)S(1)}, u32[]{:S(2)}, u32[]{:S(2)}) collective-permute-start(f32[2,2,4,8,384]{4,3,2,1,0:T(8,128)S(1)} %shard_map.71), channel_id=1, source_target_pairs={{0,64},{1,193},{2,66},{3,195},{4,68},{5,197},{6,70},{7,199},{8,72}... | collective-permute-start | bytes 589832 | tf_op jit(solution)/shard_map/ppermute | solution.py:295
  30.9 12.4 %collective-permute-start.5 = (f32[2,2,4,8,384]{4,3,2,1,0:T(8,128)S(1)}, f32[2,2,4,8,384]{4,3,2,1,0:T(8,128)S(1)}, u32[]{:S(2)}, u32[]{:S(2)}) collective-permute-start(f32[2,2,4,8,384]{4,3,2,1,0:T(8,128)S(1)} %add.7.mine), channel_id=1, source_target_pairs={{0,192},{1,65},{2,194},{3,67},{4,196},{5,69},{6,198},{7,71},{8,200... | collective-permute-start | bytes 589832 | tf_op jit(solution)/shard_map/ppermute | solution.py:295
  38.1 16.3 %collective-permute-start.1 = (f32[2,8,16,384]{3,2,1,0:T(8,128)S(1)}, f32[2,8,16,384]{3,2,1,0:T(8,128)S(1)}, u32[]{:S(2)}, u32[]{:S(2)}) collective-permute-start(f32[2,8,16,384]{3,2,1,0:T(8,128)S(1)} %add.6.mine), channel_id=1, source_target_pairs={{0,192},{1,65},{2,194},{3,67},{4,196},{5,69},{6,198},{7,71},{8,200... | collective-permute-start | bytes 1179656 | tf_op jit(solution)/shard_map/ppermute | solution.py:295
  43.9 20.0 %collective-permute-start.6 = (f32[8,4,8,384]{3,2,1,0:T(8,128)S(1)}, f32[8,4,8,384]{3,2,1,0:T(8,128)S(1)}, u32[]{:S(2)}, u32[]{:S(2)}) collective-permute-start(f32[8,4,8,384]{3,2,1,0:T(8,128)S(1)} %get-tuple-element.25), channel_id=1, source_target_pairs={{0,1},{1,2},{2,3},{3,4},{4,5},{5,6},{6,7},{7,8},{8,9},{9,10},{10,1... | collective-permute-start | bytes 1179656 | tf_op jit(solution)/shard_map/ppermute | solution.py:280
  44.2 19.6 %collective-permute-start.7 = (f32[8,4,8,384]{3,2,1,0:T(8,128)S(1)}, f32[8,4,8,384]{3,2,1,0:T(8,128)S(1)}, u32[]{:S(2)}, u32[]{:S(2)}) collective-permute-start(f32[8,4,8,384]{3,2,1,0:T(8,128)S(1)} %get-tuple-element.26), channel_id=1, source_target_pairs={{0,63},{1,0},{2,1},{3,2},{4,3},{5,4},{6,5},{7,6},{8,7},{9,8},{10,9... | collective-permute-start | bytes 1179656 | tf_op jit(solution)/shard_map/ppermute | solution.py:285

commit v3 on v2

v3 whole, which is shorter than its diff:
```python
import functools
import math

import jax
import jax.numpy as jnp
from jax import lax
from jax.experimental import pallas as pl
from jax.experimental.pallas import tpu as pltpu
from jax.sharding import PartitionSpec as P

STEPS = 4
HALO = 4
TILE_ROWS = 8
VMEM_BYTES = 16 * 1024 * 1024
MOST_VMEM_BYTES = 48 * 1024 * 1024


def shifted(values, by, axis):
    return pltpu.roll(values, by % values.shape[axis], axis)


def low_half(shape):
    return lax.broadcasted_iota(jnp.int32, shape, len(shape) - 2) < HALO


def masked_rows(face):
    last = lax.broadcasted_iota(jnp.int32, face.shape, 1) == face.shape[1] - 1
    return jnp.where(last, 0.0, face)


def diffuse(fields, zonal, merid):
    rows = lax.broadcasted_iota(jnp.int32, (TILE_ROWS, zonal.shape[1]), 0)
    kept = [None] * len(fields)
    for sweep in range(STEPS):
        zonal_flux = [zonal * (shifted(f, -1, 0) - f) for f in fields]
        merid_flux = [merid * (shifted(f, -1, 1) - f) for f in fields]
        inward = [shifted(z, 1, 0) for z in zonal_flux]
        for i, f in enumerate(fields):
            cell = jnp.where(rows < HALO, f[:8], f[16:])
            flux = jnp.where(rows < HALO, zonal_flux[i][:8], inward[i][16:])
            if sweep:
                mine = (rows == sweep) | (rows == 7 - sweep)
                cell = jnp.where(mine, cell, kept[i][0])
                flux = jnp.where(mine, flux, kept[i][1])
            kept[i] = (cell, flux)
        fields = [
            (f + (z - w)) + (g - shifted(g, 1, 1))
            for f, z, w, g in zip(fields, zonal_flux, inward, merid_flux)
        ]
    return fields, kept


def window(outer, inner, by, side):
    if by == 0:
        return outer
    rows = lax.broadcasted_iota(jnp.int32, outer.shape, 0) % HALO
    if side == 0:
        return jnp.where(rows < HALO - by, shifted(outer, -by, 0), shifted(inner, HALO - by, 0))
    return jnp.where(rows >= by, shifted(outer, by, 0), shifted(inner, by - HALO, 0))


def edge_windows(outer, own, side):
    zonal_at = 0 if side == 0 else 1
    steps = []
    for step in range(STEPS):
        zonal = window(outer[0], own[0], step + zonal_at, side)
        merid = window(outer[1], own[1], step + 1, side)
        steps.append((zonal, masked_rows(merid)))
    return steps


def diffuse_edges(halos, kept, windows, side):
    rows = lax.broadcasted_iota(jnp.int32, halos[0].shape, 0) % HALO
    inward = -1 if side == 0 else 1
    newest = rows == (HALO - 1 if side == 0 else 0)
    outer = halos
    for step in range(STEPS):
        zonal, merid = windows[step]
        turn = -inward * (HALO - 1 - step)
        cells, flux_in = [], []
        for previous, (cell, flux) in zip(outer, kept):
            cells.append(jnp.where(newest, shifted(cell, turn, 0), shifted(previous, inward, 0)))
            flux_in.append(shifted(flux, turn, 0))
        merid_flux = [merid * (shifted(c, -1, 1) - c) for c in cells]
        after = []
        for previous, cell, flux, g in zip(outer, cells, flux_in, merid_flux):
            out_flux = zonal * (cell - previous if side == 0 else previous - cell)
            in_flux = jnp.where(newest, flux, shifted(out_flux, inward, 0))
            change = in_flux - out_flux if side == 0 else out_flux - in_flux
            after.append((cell + change) + (g - shifted(g, 1, 1)))
        outer = after
    return outer


def paired_heads(first, second):
    return jnp.where(low_half(first.shape), first, shifted(second, HALO, 0))


def paired_tails(first, second):
    return jnp.where(low_half(first.shape), shifted(first, HALO, 0), second)


def paired(first, second, side):
    return (paired_heads if side == 0 else paired_tails)(first, second)


def levels_of(left, right):
    low = low_half(left.shape)
    return (
        jnp.where(low, left, shifted(right, HALO, 0)),
        jnp.where(low, shifted(left, HALO, 0), right),
    )


def pack_controls(alpha, diffusivity, head, tail):
    members, pairs = alpha.shape[0], head.shape[1]
    for f in range(members + 2):
        source, at = (alpha, f) if f < members else (diffusivity, f - members)
        for p in range(pairs):
            first, second = 2 * p, 2 * p + 1
            head[f, p] = paired_heads(source[at, first, :8], source[at, second, :8])
            tail[f, p] = paired_tails(source[at, first, 16:], source[at, second, 16:])


def localize_interior(alpha, ensemble, coeffs, out, cells, fluxes, rims):
    members, levels = alpha.shape[:2]
    low = low_half((TILE_ROWS, alpha.shape[3]))

    def one(i, carry):
        fields = [alpha[m, i] for m in range(members)]
        fields, kept = diffuse(fields, coeffs[0, i], masked_rows(coeffs[1, i]))
        for m, (cell, flux) in enumerate(kept):
            cells[m, i] = cell
            fluxes[m, i] = flux
        for t in range(2):
            for m in range(members):
                scale = ensemble[t, m, i].astype(jnp.float32)
                rims[t, m, i] = jnp.where(low, scale[:8], scale[16:])
                total = scale * fields[m] if m == 0 else total + scale * fields[m]
            out[t, i, :8] = total[8:16]
            out[t, i, 8:] = jnp.where(low, total[16:], total[:8])
        return carry

    lax.fori_loop(0, levels, one, 0)


def two(ref, pair):
    ahead = (slice(None),) * (len(ref.shape) - 3)
    return ref.at[ahead + (pl.ds(2 * pair, 2),)]


def edges_of(halos, cells, fluxes, coeffs, outer, side):
    members = cells.shape[0]
    rows = slice(0, 8) if side == 0 else slice(16, 24)
    own = [paired(coeffs[f, 0, rows], coeffs[f, 1, rows], side) for f in range(2)]
    windows = edge_windows([outer[members], outer[members + 1]], own, side)
    kept = [
        tuple(paired(k[m, 0], k[m, 1], side) for k in (cells, fluxes)) for m in range(members)
    ]
    return diffuse_edges([halos[m] for m in range(members)], kept, windows, side)


def localize_edges(left, right, cells, fluxes, coeffs, rims, out):
    members = cells.shape[0]

    def one(pair, carry):
        scale, rim = two(rims, pair), two(out, pair)
        kept = two(cells, pair), two(fluxes, pair), two(coeffs, pair)
        sides = [
            edges_of(outer.at[:, pair], *kept, outer.at[:, pair], side)
            for side, outer in enumerate((left, right))
        ]
        edges = [levels_of(sides[0][m], sides[1][m]) for m in range(members)]
        for j in range(2):
            for t in range(2):
                for m in range(members):
                    term = scale[t, m, j] * edges[m][j]
                    total = term if m == 0 else total + term
                rim[t, j] = total
        return carry

    lax.fori_loop(0, left.shape[1], one, 0)


def project_edges(mine, other, innovation, precision, rims, rim, head, tail):
    members = rims.shape[1]
    low = low_half(mine.shape[2:])

    def one(pair, carry):
        scale, out = two(rims, pair), two(rim, pair)
        parts = [two(ref, pair) for ref in (mine, other, innovation, precision)]
        edges = []
        for j in range(2):
            edge = []
            for t in range(2):
                total = parts[0][t, j] + parts[1][t, j]
                out[t, j] = total
                seen, trust = (jnp.where(low, p[t, j, :8], p[t, j, 16:]) for p in parts[2:])
                edge.append(trust * (total - seen))
            edges.append(edge)
        for m in range(members):
            first, second = (
                scale[0, m, j] * edges[j][0] + scale[1, m, j] * edges[j][1] for j in range(2)
            )
            head[m, pair] = paired_heads(first, second)
            tail[m, pair] = paired_tails(first, second)
        return carry

    lax.fori_loop(0, head.shape[1], one, 0)


def adjoint_interior(
    mine, other, rim, innovation, precision, ensemble, alpha, coeffs,
    increment, inner, cells, fluxes,
):
    members, levels = alpha.shape[:2]
    low = low_half((TILE_ROWS, alpha.shape[3]))

    def one(i, carry):
        scale, control, face = ensemble.at[:, :, i], alpha.at[:, i], coeffs.at[:, i]
        out = [ref.at[:, i] for ref in (inner, cells, fluxes)]
        weight = []
        for t in range(2):
            middle = mine[t, i] + other[t, i]
            edge, rest = rim[t, i], middle[8:]
            total = jnp.concatenate(
                [jnp.where(low, edge, rest), middle[:8], jnp.where(low, rest, edge)], axis=0
            )
            increment[t, i] = total
            weight.append(precision[t, i] * (total - innovation[t, i]))
        projected = [
            scale[0, m].astype(jnp.float32) * weight[0] + scale[1, m].astype(jnp.float32) * weight[1]
            for m in range(members)
        ]
        fields, kept = diffuse(projected, face[0], masked_rows(face[1]))
        for m, (cell, flux) in enumerate(kept):
            out[1][m] = cell
            out[2][m] = flux
            out[0][m] = control[m] + fields[m]
        return carry

    lax.fori_loop(0, levels, one, 0)


def adjoint_edges(
    inner, alpha, p_left, p_right, cells, fluxes, coeffs, left, right, increment,
    gradient, whole_increment,
):
    pair = pl.program_id(0)
    members = alpha.shape[0]
    low = low_half((TILE_ROWS, alpha.shape[3]))
    kept = two(cells, pair), two(fluxes, pair), two(coeffs, pair)
    inside, control, total = two(inner, pair), two(alpha, pair), two(increment, pair)
    sides = [
        edges_of(halos.at[:, pair], *kept, outer.at[:, pair], side)
        for side, (halos, outer) in enumerate(((p_left, left), (p_right, right)))
    ]
    for m in range(members):
        for j, edge in enumerate(levels_of(sides[0][m], sides[1][m])):
            gradient[m, j, :8] = jnp.where(low, control[m, j, :8] + edge, inside[m, j, :8])
            gradient[m, j, 8:16] = inside[m, j, 8:16]
            gradient[m, j, 16:] = jnp.where(low, inside[m, j, 16:], control[m, j, 16:] + edge)
    for t in range(2):
        for j in range(2):
            whole_increment[t, j] = total[t, j]


def f32(*shape):
    return jax.ShapeDtypeStruct(shape, jnp.float32)


def run(kernel, out_shape, flops, *args, vmem=VMEM_BYTES, **options):
    read = sum(a.size * a.dtype.itemsize for a in args)
    wrote = sum(4 * math.prod(s.shape) for s in out_shape)
    whole = pl.BlockSpec(memory_space=pltpu.VMEM)
    if "grid_spec" not in options:
        options = {"in_specs": [whole] * len(args), "out_specs": [whole] * len(out_shape)} | options
    return pl.pallas_call(
        kernel,
        out_shape=out_shape,
        cost_estimate=pl.CostEstimate(flops=flops, bytes_accessed=read + wrote, transcendentals=0),
        compiler_params=pltpu.CompilerParams(vmem_limit_bytes=vmem),
        **options,
    )(*args)


def in_vmem(value):
    return pltpu.with_memory_space_constraint(value, pltpu.VMEM)


def to_right(value):
    size = lax.axis_size("tile")
    return lax.ppermute(value, "tile", [(i, (i + 1) % size) for i in range(size)])


def to_left(value):
    size = lax.axis_size("tile")
    return lax.ppermute(value, "tile", [(i, (i - 1) % size) for i in range(size)])


def with_partner(value, first):
    mem, tile = lax.axis_size("mem"), lax.axis_size("tile")
    pairs = []
    for m in range(mem):
        for t in range(tile):
            flip = 1 if (t % 2 == 0) == first else 3
            pairs.append((m * tile + t, (m ^ flip) * tile + t))
    return lax.ppermute(value, ("mem", "tile"), pairs)


def per_device(alpha, ensemble, innovation, precision, diffusivity):
    members, levels, columns, rows = alpha.shape
    slots = ensemble.shape[0]
    pairs = levels // 2
    work = members * levels * columns * rows * 10 * STEPS

    edge = pltpu.VMEM((members + 2, pairs, TILE_ROWS, rows), jnp.float32)
    head, tail = run(pack_controls, [edge, edge], 0, alpha, diffusivity)
    left = in_vmem(to_right(tail))
    right = in_vmem(to_left(head))

    kept = f32(members, levels, TILE_ROWS, rows)
    part_mid, cells, fluxes, rims = run(
        localize_interior,
        [f32(slots, levels, 16, rows), kept, kept, f32(slots, members, levels, TILE_ROWS, rows)],
        work, alpha, ensemble, diffusivity, vmem=MOST_VMEM_BYTES,
    )
    got_mid = with_partner(part_mid, True)
    (part_rim,) = run(
        localize_edges, [f32(slots, levels, TILE_ROWS, rows)], work // 3,
        left, right, cells, fluxes, diffusivity, rims,
    )
    got_rim = with_partner(part_rim, True)
    half_mid = part_mid + got_mid
    other_mid = with_partner(half_mid, False)
    half_rim = part_rim + got_rim
    other_rim = with_partner(half_rim, False)

    p_edge = f32(members, pairs, TILE_ROWS, rows)
    rim, p_head, p_tail = run(
        project_edges, [f32(slots, levels, TILE_ROWS, rows), p_edge, p_edge], 0,
        half_rim, other_rim, innovation, precision, rims,
    )
    p_left = to_right(p_tail)
    p_right = to_left(p_head)

    obs, field = f32(*innovation.shape), f32(*alpha.shape)
    increment, inner, cells, fluxes = run(
        adjoint_interior, [obs, field, kept, kept], work,
        half_mid, other_mid, rim, innovation, precision, ensemble, alpha, diffusivity,
    )
    args = (inner, alpha, p_left, p_right, cells, fluxes, diffusivity, left, right, increment)
    return tuple(
        run(
            adjoint_edges, [field, obs], work // 3, *args,
            grid=(pairs,),
            out_specs=[
                pl.BlockSpec((members, 2, columns, rows), lambda i: (0, i, 0, 0)),
                pl.BlockSpec((slots, 2, columns, rows), lambda i: (0, i, 0, 0)),
            ],
        )
    )


def solution(mesh):
    in_specs = (
        P("mem", None, "tile", None),
        P(None, "mem", None, "tile", None),
        P(None, None, "tile", None),
        P(None, None, "tile", None),
        P(None, None, "tile", None),
    )
    out_specs = (P("mem", None, "tile", None), P(None, None, "tile", None))
    return jax.shard_map(
        per_device, mesh=mesh, in_specs=in_specs, out_specs=out_specs, check_vma=False
    )
```

time: 70.1 us -> 64 us (0.913)
  the two profiles are of different devices: /device:TPU:22 before, /device:TPU:0 now
where the time goes in v3:
time: 64 us; the launch traced here: 63 us
  Pallas kernels  22.2 us (35%)
  starting transfers between devices  19.6 us (31%)
  waiting for transfers between devices  17.7 us (28%)
  local copies, waits for them, and re-layouts  2.75 us (4%)
  between operations  0.73 us (1%)
    pallas_call x6, Pallas kernels, run(): pl.pallas_call(kernel, out_shape=out_shape, cost_estimate=pl.CostEstimate...  22.2 us
    ppermute x4, waiting for transfers between devices, with_partner(): return lax.ppermute(value, ('mem', 'tile'), pairs)  17.4 us
    ppermute x2, starting transfers between devices, to_left(): lax.ppermute(value, 'tile', [(i, (i - 1) % size) for i in range(size)])  10.9 us
    ppermute x4, starting transfers between devices, with_partner(): return lax.ppermute(value, ('mem', 'tile'), pairs)  7.54 us
    unnamed x14, local copies, waits for them, and re-layouts  2.75 us
  transfers between devices with their start and end apart: 8, of which 4 were waited for; matrix products, arithmetic and copies ran while one was open for 0% of the time, Pallas kernels for 29%

profile of v3, /device:TPU:0, one launch (start us, length us, event | category | flops | bytes accessed | tf_op | source)
XLA Modules:
  0.0 63.0 jit_solution(4364441409024458208)
XLA Ops:
  0.6 0.0 copy-start
  0.6 1.7 %copy-done = f32[8,8,24,384]{3,2,1,0:T(8,128)S(1)} copy-done((f32[8,8,24,384]{3,2,1,0:T(8,128)S(1)}, f32[8,8,24,384]{3,2,1,0:T(8,128)}, u32[]{:S(2)}) %copy-start) | copy-done | bytes 2359320
  2.3 1.1 %copy-done.2 = f32[2,8,24,384]{3,2,1,0:T(8,128)S(1)} copy-done((f32[2,8,24,384]{3,2,1,0:T(8,128)S(1)}, f32[2,8,24,384]{3,2,1,0:T(8,128)}, u32[]{:S(2)}) %copy-start.2) | copy-done | bytes 589848
  3.4 0.1 shard_map.69
  3.5 0.1 collective-permute-start.2
  3.6 6.0 %collective-permute-start.3 = (f32[10,4,8,384]{3,2,1,0:T(8,128)S(1)}, f32[10,4,8,384]{3,2,1,0:T(8,128)S(1)}, u32[]{:S(2)}, u32[]{:S(2)}) collective-permute-start(f32[10,4,8,384]{3,2,1,0:T(8,128)S(1)} %get-tuple-element.17), channel_id=1, source_target_pairs={{0,63},{1,0},{2,1},{3,2},{4,3},{5,4},{6,5},{7,6},{8,7},{9,8},{10,9... | collective-permute-start | bytes 1474568 | tf_op jit(solution)/shard_map/ppermute | solution.py:298
  9.5 8.9 %shard_map.68 = (f32[2,8,16,384]{3,2,1,0:T(8,128)S(1)}, f32[8,8,8,384]{3,2,1,0:T(8,128)S(1)}, f32[8,8,8,384]{3,2,1,0:T(8,128)S(1)}, f32[2,8,8,8,384]{4,3,2,1,0:T(8,128)S(1)}) custom-call(f32[8,8,24,384]{3,2,1,0:T(8,128)} %alpha.7, bf16[2,8,8,24,384]{4,3,2,1,0:T(8,128)(2,1)} %ensemble.3, f32[2,8,24,384]{3,2,1,0:T(8,128)S(1)} %copy-done.3), custom_call_target="tpu_custom_call" | custom-call | flops 23592960 | bytes 8847360 | tf_op jit(solution)/shard_map/pallas_call | solution.py:278
  18.4 1.7 %collective-permute-start = (f32[2,8,16,384]{3,2,1,0:T(8,128)S(1)}, f32[2,8,16,384]{3,2,1,0:T(8,128)S(1)}, u32[]{:S(2)}, u32[]{:S(2)}) collective-permute-start(f32[2,8,16,384]{3,2,1,0:T(8,128)S(1)} %get-tuple-element.15), channel_id=1, source_target_pairs={{0,64},{1,193},{2,66},{3,195},{4,68},{5,197},{6,70},{7,199},{8,72}... | collective-permute-start | bytes 1179656 | tf_op jit(solution)/shard_map/ppermute | solution.py:308
  20.2 0.0 copy-start.6
  20.2 2.8 %shard_map.70 = f32[2,8,8,384]{3,2,1,0:T(8,128)S(1)} custom-call(f32[10,4,8,384]{3,2,1,0:T(8,128)S(1)} %collective-permute-done.2.left, f32[10,4,8,384]{3,2,1,0:T(8,128)S(1)} %collective-permute-done.3.right, f32[8,8,8,384]{3,2,1,0:T(8,128)S(1)} %get-tuple-element.18.cells, f32[8,8,8,384]{3,2,1,0:T(8,128)S(1)} %get-tuple-element.19.fluxes, ...), custom_call_target="tpu_custom_call" | custom-call | flops 7864320 | bytes 4915200 | tf_op jit(solution)/shard_map/pallas_call | solution.py:278
  23.0 0.0 copy-start.1
  23.0 0.0 copy-start.4
  23.0 1.4 %collective-permute-start.4 = (f32[2,8,8,384]{3,2,1,0:T(8,128)S(1)}, f32[2,8,8,384]{3,2,1,0:T(8,128)S(1)}, u32[]{:S(2)}, u32[]{:S(2)}) collective-permute-start(f32[2,8,8,384]{3,2,1,0:T(8,128)S(1)} %shard_map.70), channel_id=1, source_target_pairs={{0,64},{1,193},{2,66},{3,195},{4,68},{5,197},{6,70},{7,199},{8,72}... | collective-permute-start | bytes 589832 | tf_op jit(solution)/shard_map/ppermute | solution.py:308
  24.4 9.6 %collective-permute-done.4 = f32[2,8,8,384]{3,2,1,0:T(8,128)S(1)} collective-permute-done((f32[2,8,8,384]{3,2,1,0:T(8,128)S(1)}, f32[2,8,8,384]{3,2,1,0:T(8,128)S(1)}, u32[]{:S(2)}, u32[]{:S(2)}) %collective-permute-start.4) | collective-permute-done | bytes 196640 | tf_op jit(solution)/shard_map/ppermute | solution.py:308
  34.0 4.3 %collective-permute-start.5 = (f32[2,8,8,384]{3,2,1,0:T(8,128)S(1)}, f32[2,8,8,384]{3,2,1,0:T(8,128)S(1)}, u32[]{:S(2)}, u32[]{:S(2)}) collective-permute-start(f32[2,8,8,384]{3,2,1,0:T(8,128)S(1)} %add.7.mine), channel_id=1, source_target_pairs={{0,192},{1,65},{2,194},{3,67},{4,196},{5,69},{6,198},{7,71},{8,200... | collective-permute-start | bytes 589832 | tf_op jit(solution)/shard_map/ppermute | solution.py:308
  38.4 0.1 collective-permute-start.1
  38.5 5.1 %collective-permute-done.5.other = f32[2,8,8,384]{3,2,1,0:T(8,128)S(1)} collective-permute-done((f32[2,8,8,384]{3,2,1,0:T(8,128)S(1)}, f32[2,8,8,384]{3,2,1,0:T(8,128)S(1)}, u32[]{:S(2)}, u32[]{:S(2)}) %collective-permute-start.5) | collective-permute-done | bytes 196640 | tf_op jit(solution)/shard_map/ppermute | solution.py:308
  43.6 0.2 shard_map.71
  43.8 1.1 %collective-permute-start.6 = (f32[8,4,8,384]{3,2,1,0:T(8,128)S(1)}, f32[8,4,8,384]{3,2,1,0:T(8,128)S(1)}, u32[]{:S(2)}, u32[]{:S(2)}) collective-permute-start(f32[8,4,8,384]{3,2,1,0:T(8,128)S(1)} %get-tuple-element.23), channel_id=1, source_target_pairs={{0,1},{1,2},{2,3},{3,4},{4,5},{5,6},{6,7},{7,8},{8,9},{9,10},{10,1... | collective-permute-start | bytes 1179656 | tf_op jit(solution)/shard_map/ppermute | solution.py:293
  44.9 5.0 %collective-permute-start.7 = (f32[8,4,8,384]{3,2,1,0:T(8,128)S(1)}, f32[8,4,8,384]{3,2,1,0:T(8,128)S(1)}, u32[]{:S(2)}, u32[]{:S(2)}) collective-permute-start(f32[8,4,8,384]{3,2,1,0:T(8,128)S(1)} %get-tuple-element.24), channel_id=1, source_target_pairs={{0,63},{1,0},{2,1},{3,2},{4,3},{5,4},{6,5},{7,6},{8,7},{9,8},{10,9... | collective-permute-start | bytes 1179656 | tf_op jit(solution)/shard_map/ppermute | solution.py:298
  49.8 2.7 %collective-permute-done.1.other = f32[2,8,16,384]{3,2,1,0:T(8,128)S(1)} collective-permute-done((f32[2,8,16,384]{3,2,1,0:T(8,128)S(1)}, f32[2,8,16,384]{3,2,1,0:T(8,128)S(1)}, u32[]{:S(2)}, u32[]{:S(2)}) %collective-permute-start.1) | collective-permute-done | bytes 393248 | tf_op jit(solution)/shard_map/ppermute | solution.py:308
  52.6 6.3 %shard_map.72 = (f32[2,8,24,384]{3,2,1,0:T(8,128)S(1)}, f32[8,8,24,384]{3,2,1,0:T(8,128)S(1)}, f32[8,8,8,384]{3,2,1,0:T(8,128)S(1)}, f32[8,8,8,384]{3,2,1,0:T(8,128)S(1)}) custom-call(f32[2,8,16,384]{3,2,1,0:T(8,128)S(1)} %add.6.mine, f32[2,8,16,384]{3,2,1,0:T(8,128)S(1)} %collective-permute-done.1.other, f32[2,8,8,384]{3,2,1,0:T(8,128)S(1)} %get-tuple-element.21.rim, ...), custom_call_target="tpu_custom_call" | custom-call | flops 23592960 | bytes 11993088 | tf_op jit(solution)/shard_map/pallas_call | solution.py:278
  58.9 0.3 collective-permute-done.6.p_left
  59.2 3.9 %shard_map.73 = (f32[8,8,24,384]{3,2,1,0:T(8,128)}, f32[2,8,24,384]{3,2,1,0:T(8,128)}) custom-call(f32[8,8,24,384]{3,2,1,0:T(8,128)S(1)} %get-tuple-element.22.inner, f32[8,8,24,384]{3,2,1,0:T(8,128)S(1)} %copy-done.1, f32[8,4,8,384]{3,2,1,0:T(8,128)S(1)} %collective-permute-done.6.p_left, f32[8,4,8,384]{3,2,1,0:T(8,128)S(1)} %collective-permute-done.7.p_right, ...), custom_call_target="tpu_custom_call" | custom-call | flops 7864320 | bytes 12189696 | tf_op jit(solution)/shard_map/pallas_call | solution.py:278
  (14 shorter events, 0.1 us)
Async XLA Ops:
  0.6 1.7 %copy-start = (f32[8,8,24,384]{3,2,1,0:T(8,128)S(1)}, f32[8,8,24,384]{3,2,1,0:T(8,128)}, u32[]{:S(2)}) copy-start(f32[8,8,24,384]{3,2,1,0:T(8,128)} %alpha.7) | copy-start | bytes 7077892
  2.3 1.1 %copy-start.2 = (f32[2,8,24,384]{3,2,1,0:T(8,128)S(1)}, f32[2,8,24,384]{3,2,1,0:T(8,128)}, u32[]{:S(2)}) copy-start(f32[2,8,24,384]{3,2,1,0:T(8,128)} %coeffs.7) | copy-start | bytes 1769476
  3.4 6.1 %copy-start.3 = (f32[2,8,24,384]{3,2,1,0:T(8,128)S(1)}, f32[2,8,24,384]{3,2,1,0:T(8,128)}, u32[]{:S(2)}) copy-start(f32[2,8,24,384]{3,2,1,0:T(8,128)} %coeffs.7) | copy-start | bytes 1769476
  3.5 16.7 %collective-permute-start.2 = (f32[10,4,8,384]{3,2,1,0:T(8,128)S(1)}, f32[10,4,8,384]{3,2,1,0:T(8,128)S(1)}, u32[]{:S(2)}, u32[]{:S(2)}) collective-permute-start(f32[10,4,8,384]{3,2,1,0:T(8,128)S(1)} %get-tuple-element.16), channel_id=1, source_target_pairs={{0,1},{1,2},{2,3},{3,4},{4,5},{5,6},{6,7},{7,8},{8,9},{9,10},{10,1... | collective-permute-start | bytes 1474568 | tf_op jit(solution)/shard_map/ppermute | solution.py:293
  3.6 16.6 %collective-permute-start.3 = (f32[10,4,8,384]{3,2,1,0:T(8,128)S(1)}, f32[10,4,8,384]{3,2,1,0:T(8,128)S(1)}, u32[]{:S(2)}, u32[]{:S(2)}) collective-permute-start(f32[10,4,8,384]{3,2,1,0:T(8,128)S(1)} %get-tuple-element.17), channel_id=1, source_target_pairs={{0,63},{1,0},{2,1},{3,2},{4,3},{5,4},{6,5},{7,6},{8,7},{9,8},{10,9... | collective-permute-start | bytes 1474568 | tf_op jit(solution)/shard_map/ppermute | solution.py:298
  18.4 19.9 %collective-permute-start = (f32[2,8,16,384]{3,2,1,0:T(8,128)S(1)}, f32[2,8,16,384]{3,2,1,0:T(8,128)S(1)}, u32[]{:S(2)}, u32[]{:S(2)}) collective-permute-start(f32[2,8,16,384]{3,2,1,0:T(8,128)S(1)} %get-tuple-element.15), channel_id=1, source_target_pairs={{0,64},{1,193},{2,66},{3,195},{4,68},{5,197},{6,70},{7,199},{8,72}... | collective-permute-start | bytes 1179656 | tf_op jit(solution)/shard_map/ppermute | solution.py:308
  20.2 23.4 %copy-start.5 = (f32[2,8,24,384]{3,2,1,0:T(8,128)S(1)}, f32[2,8,24,384]{3,2,1,0:T(8,128)}, u32[]{:S(2)}) copy-start(f32[2,8,24,384]{3,2,1,0:T(8,128)} %innovation.3) | copy-start | bytes 1769476
  20.2 23.4 %copy-start.6 = (f32[2,8,24,384]{3,2,1,0:T(8,128)S(1)}, f32[2,8,24,384]{3,2,1,0:T(8,128)}, u32[]{:S(2)}) copy-start(f32[2,8,24,384]{3,2,1,0:T(8,128)} %precision.3) | copy-start | bytes 1769476
  23.0 29.6 %copy-start.1 = (f32[8,8,24,384]{3,2,1,0:T(8,128)S(1)}, f32[8,8,24,384]{3,2,1,0:T(8,128)}, u32[]{:S(2)}) copy-start(f32[8,8,24,384]{3,2,1,0:T(8,128)} %alpha.7) | copy-start | bytes 7077892
  23.0 29.6 %copy-start.4 = (bf16[2,8,8,24,384]{4,3,2,1,0:T(8,128)(2,1)S(1)}, bf16[2,8,8,24,384]{4,3,2,1,0:T(8,128)(2,1)}, u32[]{:S(2)}) copy-start(bf16[2,8,8,24,384]{4,3,2,1,0:T(8,128)(2,1)} %ensemble.3) | copy-start | bytes 7077892
  23.0 10.9 %collective-permute-start.4 = (f32[2,8,8,384]{3,2,1,0:T(8,128)S(1)}, f32[2,8,8,384]{3,2,1,0:T(8,128)S(1)}, u32[]{:S(2)}, u32[]{:S(2)}) collective-permute-start(f32[2,8,8,384]{3,2,1,0:T(8,128)S(1)} %shard_map.70), channel_id=1, source_target_pairs={{0,64},{1,193},{2,66},{3,195},{4,68},{5,197},{6,70},{7,199},{8,72}... | collective-permute-start | bytes 589832 | tf_op jit(solution)/shard_map/ppermute | solution.py:308
  34.0 9.6 %collective-permute-start.5 = (f32[2,8,8,384]{3,2,1,0:T(8,128)S(1)}, f32[2,8,8,384]{3,2,1,0:T(8,128)S(1)}, u32[]{:S(2)}, u32[]{:S(2)}) collective-permute-start(f32[2,8,8,384]{3,2,1,0:T(8,128)S(1)} %add.7.mine), channel_id=1, source_target_pairs={{0,192},{1,65},{2,194},{3,67},{4,196},{5,69},{6,198},{7,71},{8,200... | collective-permute-start | bytes 589832 | tf_op jit(solution)/shard_map/ppermute | solution.py:308
  38.4 14.2 %collective-permute-start.1 = (f32[2,8,16,384]{3,2,1,0:T(8,128)S(1)}, f32[2,8,16,384]{3,2,1,0:T(8,128)S(1)}, u32[]{:S(2)}, u32[]{:S(2)}) collective-permute-start(f32[2,8,16,384]{3,2,1,0:T(8,128)S(1)} %add.6.mine), channel_id=1, source_target_pairs={{0,192},{1,65},{2,194},{3,67},{4,196},{5,69},{6,198},{7,71},{8,200... | collective-permute-start | bytes 1179656 | tf_op jit(solution)/shard_map/ppermute | solution.py:308
  43.8 15.4 %collective-permute-start.6 = (f32[8,4,8,384]{3,2,1,0:T(8,128)S(1)}, f32[8,4,8,384]{3,2,1,0:T(8,128)S(1)}, u32[]{:S(2)}, u32[]{:S(2)}) collective-permute-start(f32[8,4,8,384]{3,2,1,0:T(8,128)S(1)} %get-tuple-element.23), channel_id=1, source_target_pairs={{0,1},{1,2},{2,3},{3,4},{4,5},{5,6},{6,7},{7,8},{8,9},{9,10},{10,1... | collective-permute-start | bytes 1179656 | tf_op jit(solution)/shard_map/ppermute | solution.py:293
  44.9 14.3 %collective-permute-start.7 = (f32[8,4,8,384]{3,2,1,0:T(8,128)S(1)}, f32[8,4,8,384]{3,2,1,0:T(8,128)S(1)}, u32[]{:S(2)}, u32[]{:S(2)}) collective-permute-start(f32[8,4,8,384]{3,2,1,0:T(8,128)S(1)} %get-tuple-element.24), channel_id=1, source_target_pairs={{0,63},{1,0},{2,1},{3,2},{4,3},{5,4},{6,5},{7,6},{8,7},{9,8},{10,9... | collective-permute-start | bytes 1179656 | tf_op jit(solution)/shard_map/ppermute | solution.py:298
